TPU v7x, 512 devices: a whole 4x8x8 slice. The times are simulated.
512 devices in a mesh: samp: 4 (over x_lo, core), var: 128 (over y, z, x_hi).
Axes of the slice: x: 4 (x_hi: 2, x_lo: 2; x = x_hi * 2 + x_lo), y: 8, z: 8, core: 2. Of those that a mesh axis runs over, the one named last changes fastest.
Arguments:
- genotypes: int32 [256, 16384], P('samp', 'var'), may hold values from 0 to 2
- covariates: float32 [256, 40], P('samp'), may hold values from -6 to 6
- traits: float32 [256, 8], P('samp'), may hold values from -6 to 6
- trait_weights: float32 [8], replicated, may hold values from 0.25 to 2
Outputs:
- block_scores: float32 [16384, 128], P('var')
All inputs are finite; a program needn't handle non-finite values.
Results may differ from a plain program's by a relative error of at most 0.0003.
Values sent between devices are 32-bit elements; how exact they have to be, the bound alone decides.
A program may use at most 64 MiB of HBM per device.

v0:
```python
import math

import jax
import jax.numpy as jnp
from jax import lax
from jax.sharding import PartitionSpec as P


def from_behind(block, axis, distance):
    devices = range(lax.axis_size(axis))
    route = [((i - distance) % len(devices), i) for i in devices]
    return lax.ppermute(block, axis, route)


def body(genotypes, covariates, traits, trait_weights):
    highest = lax.Precision.HIGHEST
    samp_count = lax.axis_size("samp")
    var_count = lax.axis_size("var")
    half_loop = var_count // 2
    section = lax.axis_index("samp")
    var_block = lax.axis_index("var")
    cov_count = covariates.shape[1]
    block_width = genotypes.shape[1]
    trait_count = traits.shape[1]
    samples = genotypes.shape[0] * samp_count
    row_count = block_width // samp_count
    centred = genotypes.astype(jnp.float32) - 1.0
    cross_part = jnp.dot(covariates.T, covariates, precision=highest)
    gene_part = jnp.dot(covariates.T, centred, precision=highest)
    trait_part = jnp.dot(covariates.T, traits, precision=highest)
    cross, gene_rhs, trait_rhs = lax.psum((cross_part, gene_part, trait_part), "samp")
    cross = cross + samples / 10.0 * jnp.eye(cov_count, dtype=jnp.float32)
    factor = jnp.linalg.cholesky(cross)
    coef_g = jax.scipy.linalg.cho_solve((factor, True), gene_rhs)
    coef_y = jax.scipy.linalg.cho_solve((factor, True), trait_rhs)
    resid_local = centred - jnp.dot(covariates, coef_g, precision=highest)
    scaled_local = (traits - jnp.dot(covariates, coef_y, precision=highest)) * (
        1.0 / math.sqrt(samples)
    )
    gathered, yscaled = (
        lax.all_gather(resid_local, "samp", axis=0, tiled=True),
        lax.all_gather(scaled_local, "samp", axis=0, tiled=True),
    )
    mine = lax.dynamic_slice_in_dim(gathered, section * row_count, row_count, 1)
    weighted = mine[:, None, :] * yscaled[:, :, None]
    weighted = weighted.reshape(samples, trait_count * row_count)

    def pair_terms(panel):
        statistic = lax.dot_general(
            weighted,
            panel,
            (((0,), (0,)), ((), ())),
            precision=highest,
            preferred_element_type=jnp.float32,
        )
        statistic = statistic.reshape(trait_count, row_count, block_width)
        return jnp.tensordot(trait_weights, statistic * statistic, axes=1, precision=highest)

    first = pair_terms(gathered)
    row_ids = section * row_count + lax.broadcasted_iota(jnp.int32, (row_count, block_width), 0)
    col_ids = lax.broadcasted_iota(jnp.int32, (row_count, block_width), 1)
    first = jnp.where(row_ids == col_ids, 0.0, first)
    row_scores = (
        jnp.zeros((row_count, var_count), jnp.float32).at[:, var_block].set(jnp.sum(first, axis=1))
    )
    carried = jnp.zeros((half_loop - 1, block_width), jnp.float32)
    moving = gathered

    def turn(offset, carry):
        moving, row_scores, carried = carry
        moving = from_behind(moving, "var", 1)
        carried = from_behind(carried, "var", 1)
        pair_stat = pair_terms(moving)
        target = (var_block - offset) % var_count
        row_scores = row_scores.at[:, target].set(jnp.sum(pair_stat, axis=1))
        keep_cols = jnp.where(offset < half_loop, 1.0, 0.0).astype(jnp.float32)
        slot = jnp.minimum(offset - 1, half_loop - 2)
        carried = carried.at[slot].add(jnp.sum(pair_stat, axis=0) * keep_cols)
        return (moving, row_scores, carried)

    moving, row_scores, carried = lax.fori_loop(
        1, half_loop + 1, turn, (moving, row_scores, carried)
    )
    returned = from_behind(carried, "var", half_loop)
    sources = (var_block + jnp.arange(1, half_loop, dtype=jnp.int32)) % var_count
    col_part = jnp.zeros((var_count, block_width), jnp.float32).at[sources].set(returned)
    own_rows = lax.dynamic_update_slice_in_dim(
        jnp.zeros((block_width, var_count), jnp.float32), row_scores, section * row_count, 0
    )
    total = own_rows + col_part.T
    return lax.psum(total, "samp") / block_width


def solution(mesh):
    placed = (P("samp", "var"), P("samp", None), P("samp", None), P())
    return jax.shard_map(
        body, mesh=mesh, in_specs=placed, out_specs=P("var", None), check_vma=False
    )
```

profile of v0, /device:TPU:1, one launch (start us, length us, event | category | flops | bytes accessed | tf_op | source)
XLA Modules:
  0.0 1070.0 jit_solution(517148785286428137)
XLA Ops:
  8.3 16.6 %all-reduce = (f32[40,128]{1,0:T(8,128)S(1)}, f32[40,40]{1,0:T(8,128)S(1)}, f32[40,8]{0,1:T(8,128)S(1)}) all-reduce(f32[40,128]{1,0:T(8,128)S(1)} %convolution_bitcast_fusion.1, f32[40,40]{1,0:T(8,128)S(1)} %fusion.36, f32[40,8]{0,1:T(8,128)S(1)} %fusion.37), channel_id=1, replica_groups=mesh['samp'=4,'var'=128] {'samp'}, use_global_device_ids=true, to_apply=%region_3.4 | all-reduce | flops 7040 | bytes 56320 | tf_op jit(solution)/shard_map/psum | solution.py:31
  33.6 6.1 all_gather.6
  48.8 893.1 %while.25 = (s32[]{:T(128)}, f32[256,128]{1,0:T(8,128)S(1)}, f32[32,128]{0,1:T(8,128)S(1)}, f32[63,128]{1,0:T(8,128)S(1)}, s32[]{:T(128)}, /*index=5*/f32[8]{0:T...) while((s32[]{:T(128)}, f32[256,128]{1,0:T(8,128)S(1)}, ...), condition=%wide.region_12.13_spmd.clone, body=%wide.region_7.12_spmd.clone.sunk | while | flops 101163296 | bytes 1975604 | solution.py:81
  54.8 9.3 collective-permute-done
  71.7 6.0 collective-permute-done
  85.4 6.0 collective-permute-done
  99.1 6.0 collective-permute-done
  112.7 6.0 collective-permute-done
  126.4 6.0 collective-permute-done
  140.1 6.0 collective-permute-done
  153.7 6.0 collective-permute-done
  167.4 6.0 collective-permute-done
  181.0 6.0 collective-permute-done
  194.7 6.0 collective-permute-done
  208.4 6.4 collective-permute-done
  222.4 7.0 collective-permute-done
  237.1 7.6 collective-permute-done
  252.3 6.6 collective-permute-done
  266.6 6.0 collective-permute-done
  280.3 6.0 collective-permute-done
  293.9 6.0 collective-permute-done
  307.6 6.0 collective-permute-done
  321.3 6.0 collective-permute-done
  334.9 6.0 collective-permute-done
  348.6 6.0 collective-permute-done
  362.3 6.0 collective-permute-done
  375.9 6.0 collective-permute-done
  389.6 6.1 collective-permute-done
  403.3 6.6 collective-permute-done
  417.6 7.6 collective-permute-done
  432.9 7.4 collective-permute-done
  448.0 6.0 collective-permute-done
  461.7 6.0 collective-permute-done
  475.3 6.0 collective-permute-done
  489.0 6.0 collective-permute-done
  502.7 6.0 collective-permute-done
  516.3 6.0 collective-permute-done
  530.0 6.0 collective-permute-done
  543.7 6.0 collective-permute-done
  557.3 6.0 collective-permute-done
  571.0 6.0 collective-permute-done
  584.7 6.4 collective-permute-done
  598.7 7.0 collective-permute-done
  613.3 7.6 collective-permute-done
  628.6 6.7 collective-permute-done
  643.0 6.0 collective-permute-done
  656.7 6.0 collective-permute-done
  670.4 6.0 collective-permute-done
  684.0 6.0 collective-permute-done
  697.7 6.0 collective-permute-done
  711.4 6.0 collective-permute-done
  725.0 6.0 collective-permute-done
  738.7 6.0 collective-permute-done
  752.3 6.0 collective-permute-done
  766.0 6.1 collective-permute-done
  779.8 6.6 collective-permute-done
  794.1 7.6 collective-permute-done
  809.3 7.4 collective-permute-done
  824.4 6.0 collective-permute-done
  838.0 6.0 collective-permute-done
  851.7 6.0 collective-permute-done
  865.3 6.0 collective-permute-done
  920.0 6.0 collective-permute-done
  952.9 108.7 %all-reduce.3.cloned.1.call-done = f32[128,128]{0,1:T(8,128)} async-done(((f32[128,128]{0,1:T(8,128)}), f32[128,128]{0,1:T(8,128)}) %all-reduce.3.cloned.1.call-update) | async-done | bytes 65552 | tf_op jit(solution)/shard_map/psum | solution.py:91
  (1018 shorter events, 538.8 us)
Async XLA Ops:
  6.5 1055.0 %all-reduce.3.cloned.1.call-start = ((), (), s32[]{:S(2)}) async-start(), calls=%async_computation | async-start | bytes 131072 | tf_op jit(solution)/shard_map/psum | solution.py:91
  48.8 15.3 %collective-permute-start = (f32[256,128]{1,0:T(8,128)S(1)}, f32[256,128]{1,0:T(8,128)S(1)}, u32[]{:S(2)}, u32[]{:S(2)}) collective-permute-start(f32[256,128]{1,0:T(8,128)S(1)} %get-tuple-element.432), channel_id=1, source_target_pairs={{127,0},{0,1},{1,2},{2,3},{3,4},{4,5},{5,6},{6,7},{7,8},{8,9},{9,1... | collective-permute-start | bytes 393224 | tf_op jit(solution)/shard_map/while/body/eval_jaxpr/ppermute | solution.py:12
  50.7 14.9 %collective-permute-start.1 = (f32[63,128]{1,0:T(8,128)S(1)}, f32[63,128]{1,0:T(8,128)S(1)}, u32[]{:S(2)}, u32[]{:S(2)}) collective-permute-start(f32[63,128]{1,0:T(8,128)S(1)} %get-tuple-element.434), channel_id=1, source_target_pairs={{127,0},{0,1},{1,2},{2,3},{3,4},{4,5},{5,6},{6,7},{7,8},{8,9},{9,1... | collective-permute-start | bytes 96776 | tf_op jit(solution)/shard_map/while/body/eval_jaxpr/ppermute | solution.py:12
  66.3 11.4 %collective-permute-start = (f32[256,128]{1,0:T(8,128)S(1)}, f32[256,128]{1,0:T(8,128)S(1)}, u32[]{:S(2)}, u32[]{:S(2)}) collective-permute-start(f32[256,128]{1,0:T(8,128)S(1)} %get-tuple-element.432), channel_id=1, source_target_pairs={{127,0},{0,1},{1,2},{2,3},{3,4},{4,5},{5,6},{6,7},{7,8},{8,9},{9,1... | collective-permute-start | bytes 393224 | tf_op jit(solution)/shard_map/while/body/eval_jaxpr/ppermute | solution.py:12
  80.0 11.4 %collective-permute-start = (f32[256,128]{1,0:T(8,128)S(1)}, f32[256,128]{1,0:T(8,128)S(1)}, u32[]{:S(2)}, u32[]{:S(2)}) collective-permute-start(f32[256,128]{1,0:T(8,128)S(1)} %get-tuple-element.432), channel_id=1, source_target_pairs={{127,0},{0,1},{1,2},{2,3},{3,4},{4,5},{5,6},{6,7},{7,8},{8,9},{9,1... | collective-permute-start | bytes 393224 | tf_op jit(solution)/shard_map/while/body/eval_jaxpr/ppermute | solution.py:12
  93.6 11.4 %collective-permute-start = (f32[256,128]{1,0:T(8,128)S(1)}, f32[256,128]{1,0:T(8,128)S(1)}, u32[]{:S(2)}, u32[]{:S(2)}) collective-permute-start(f32[256,128]{1,0:T(8,128)S(1)} %get-tuple-element.432), channel_id=1, source_target_pairs={{127,0},{0,1},{1,2},{2,3},{3,4},{4,5},{5,6},{6,7},{7,8},{8,9},{9,1... | collective-permute-start | bytes 393224 | tf_op jit(solution)/shard_map/while/body/eval_jaxpr/ppermute | solution.py:12
  107.3 11.4 %collective-permute-start = (f32[256,128]{1,0:T(8,128)S(1)}, f32[256,128]{1,0:T(8,128)S(1)}, u32[]{:S(2)}, u32[]{:S(2)}) collective-permute-start(f32[256,128]{1,0:T(8,128)S(1)} %get-tuple-element.432), channel_id=1, source_target_pairs={{127,0},{0,1},{1,2},{2,3},{3,4},{4,5},{5,6},{6,7},{7,8},{8,9},{9,1... | collective-permute-start | bytes 393224 | tf_op jit(solution)/shard_map/while/body/eval_jaxpr/ppermute | solution.py:12
  121.0 11.4 %collective-permute-start = (f32[256,128]{1,0:T(8,128)S(1)}, f32[256,128]{1,0:T(8,128)S(1)}, u32[]{:S(2)}, u32[]{:S(2)}) collective-permute-start(f32[256,128]{1,0:T(8,128)S(1)} %get-tuple-element.432), channel_id=1, source_target_pairs={{127,0},{0,1},{1,2},{2,3},{3,4},{4,5},{5,6},{6,7},{7,8},{8,9},{9,1... | collective-permute-start | bytes 393224 | tf_op jit(solution)/shard_map/while/body/eval_jaxpr/ppermute | solution.py:12
  134.6 11.4 %collective-permute-start = (f32[256,128]{1,0:T(8,128)S(1)}, f32[256,128]{1,0:T(8,128)S(1)}, u32[]{:S(2)}, u32[]{:S(2)}) collective-permute-start(f32[256,128]{1,0:T(8,128)S(1)} %get-tuple-element.432), channel_id=1, source_target_pairs={{127,0},{0,1},{1,2},{2,3},{3,4},{4,5},{5,6},{6,7},{7,8},{8,9},{9,1... | collective-permute-start | bytes 393224 | tf_op jit(solution)/shard_map/while/body/eval_jaxpr/ppermute | solution.py:12
  148.3 11.4 %collective-permute-start = (f32[256,128]{1,0:T(8,128)S(1)}, f32[256,128]{1,0:T(8,128)S(1)}, u32[]{:S(2)}, u32[]{:S(2)}) collective-permute-start(f32[256,128]{1,0:T(8,128)S(1)} %get-tuple-element.432), channel_id=1, source_target_pairs={{127,0},{0,1},{1,2},{2,3},{3,4},{4,5},{5,6},{6,7},{7,8},{8,9},{9,1... | collective-permute-start | bytes 393224 | tf_op jit(solution)/shard_map/while/body/eval_jaxpr/ppermute | solution.py:12
  161.9 11.4 %collective-permute-start = (f32[256,128]{1,0:T(8,128)S(1)}, f32[256,128]{1,0:T(8,128)S(1)}, u32[]{:S(2)}, u32[]{:S(2)}) collective-permute-start(f32[256,128]{1,0:T(8,128)S(1)} %get-tuple-element.432), channel_id=1, source_target_pairs={{127,0},{0,1},{1,2},{2,3},{3,4},{4,5},{5,6},{6,7},{7,8},{8,9},{9,1... | collective-permute-start | bytes 393224 | tf_op jit(solution)/shard_map/while/body/eval_jaxpr/ppermute | solution.py:12
  175.6 11.4 %collective-permute-start = (f32[256,128]{1,0:T(8,128)S(1)}, f32[256,128]{1,0:T(8,128)S(1)}, u32[]{:S(2)}, u32[]{:S(2)}) collective-permute-start(f32[256,128]{1,0:T(8,128)S(1)} %get-tuple-element.432), channel_id=1, source_target_pairs={{127,0},{0,1},{1,2},{2,3},{3,4},{4,5},{5,6},{6,7},{7,8},{8,9},{9,1... | collective-permute-start | bytes 393224 | tf_op jit(solution)/shard_map/while/body/eval_jaxpr/ppermute | solution.py:12
  189.3 11.4 %collective-permute-start = (f32[256,128]{1,0:T(8,128)S(1)}, f32[256,128]{1,0:T(8,128)S(1)}, u32[]{:S(2)}, u32[]{:S(2)}) collective-permute-start(f32[256,128]{1,0:T(8,128)S(1)} %get-tuple-element.432), channel_id=1, source_target_pairs={{127,0},{0,1},{1,2},{2,3},{3,4},{4,5},{5,6},{6,7},{7,8},{8,9},{9,1... | collective-permute-start | bytes 393224 | tf_op jit(solution)/shard_map/while/body/eval_jaxpr/ppermute | solution.py:12
  202.9 11.8 %collective-permute-start = (f32[256,128]{1,0:T(8,128)S(1)}, f32[256,128]{1,0:T(8,128)S(1)}, u32[]{:S(2)}, u32[]{:S(2)}) collective-permute-start(f32[256,128]{1,0:T(8,128)S(1)} %get-tuple-element.432), channel_id=1, source_target_pairs={{127,0},{0,1},{1,2},{2,3},{3,4},{4,5},{5,6},{6,7},{7,8},{8,9},{9,1... | collective-permute-start | bytes 393224 | tf_op jit(solution)/shard_map/while/body/eval_jaxpr/ppermute | solution.py:12
  217.0 12.5 %collective-permute-start = (f32[256,128]{1,0:T(8,128)S(1)}, f32[256,128]{1,0:T(8,128)S(1)}, u32[]{:S(2)}, u32[]{:S(2)}) collective-permute-start(f32[256,128]{1,0:T(8,128)S(1)} %get-tuple-element.432), channel_id=1, source_target_pairs={{127,0},{0,1},{1,2},{2,3},{3,4},{4,5},{5,6},{6,7},{7,8},{8,9},{9,1... | collective-permute-start | bytes 393224 | tf_op jit(solution)/shard_map/while/body/eval_jaxpr/ppermute | solution.py:12
  218.9 12.0 %collective-permute-start.1 = (f32[63,128]{1,0:T(8,128)S(1)}, f32[63,128]{1,0:T(8,128)S(1)}, u32[]{:S(2)}, u32[]{:S(2)}) collective-permute-start(f32[63,128]{1,0:T(8,128)S(1)} %get-tuple-element.434), channel_id=1, source_target_pairs={{127,0},{0,1},{1,2},{2,3},{3,4},{4,5},{5,6},{6,7},{7,8},{8,9},{9,1... | collective-permute-start | bytes 96776 | tf_op jit(solution)/shard_map/while/body/eval_jaxpr/ppermute | solution.py:12
  231.6 13.0 %collective-permute-start = (f32[256,128]{1,0:T(8,128)S(1)}, f32[256,128]{1,0:T(8,128)S(1)}, u32[]{:S(2)}, u32[]{:S(2)}) collective-permute-start(f32[256,128]{1,0:T(8,128)S(1)} %get-tuple-element.432), channel_id=1, source_target_pairs={{127,0},{0,1},{1,2},{2,3},{3,4},{4,5},{5,6},{6,7},{7,8},{8,9},{9,1... | collective-permute-start | bytes 393224 | tf_op jit(solution)/shard_map/while/body/eval_jaxpr/ppermute | solution.py:12
  233.6 12.6 %collective-permute-start.1 = (f32[63,128]{1,0:T(8,128)S(1)}, f32[63,128]{1,0:T(8,128)S(1)}, u32[]{:S(2)}, u32[]{:S(2)}) collective-permute-start(f32[63,128]{1,0:T(8,128)S(1)} %get-tuple-element.434), channel_id=1, source_target_pairs={{127,0},{0,1},{1,2},{2,3},{3,4},{4,5},{5,6},{6,7},{7,8},{8,9},{9,1... | collective-permute-start | bytes 96776 | tf_op jit(solution)/shard_map/while/body/eval_jaxpr/ppermute | solution.py:12
  246.9 12.1 %collective-permute-start = (f32[256,128]{1,0:T(8,128)S(1)}, f32[256,128]{1,0:T(8,128)S(1)}, u32[]{:S(2)}, u32[]{:S(2)}) collective-permute-start(f32[256,128]{1,0:T(8,128)S(1)} %get-tuple-element.432), channel_id=1, source_target_pairs={{127,0},{0,1},{1,2},{2,3},{3,4},{4,5},{5,6},{6,7},{7,8},{8,9},{9,1... | collective-permute-start | bytes 393224 | tf_op jit(solution)/shard_map/while/body/eval_jaxpr/ppermute | solution.py:12
  248.8 11.6 %collective-permute-start.1 = (f32[63,128]{1,0:T(8,128)S(1)}, f32[63,128]{1,0:T(8,128)S(1)}, u32[]{:S(2)}, u32[]{:S(2)}) collective-permute-start(f32[63,128]{1,0:T(8,128)S(1)} %get-tuple-element.434), channel_id=1, source_target_pairs={{127,0},{0,1},{1,2},{2,3},{3,4},{4,5},{5,6},{6,7},{7,8},{8,9},{9,1... | collective-permute-start | bytes 96776 | tf_op jit(solution)/shard_map/while/body/eval_jaxpr/ppermute | solution.py:12
  261.2 11.4 %collective-permute-start = (f32[256,128]{1,0:T(8,128)S(1)}, f32[256,128]{1,0:T(8,128)S(1)}, u32[]{:S(2)}, u32[]{:S(2)}) collective-permute-start(f32[256,128]{1,0:T(8,128)S(1)} %get-tuple-element.432), channel_id=1, source_target_pairs={{127,0},{0,1},{1,2},{2,3},{3,4},{4,5},{5,6},{6,7},{7,8},{8,9},{9,1... | collective-permute-start | bytes 393224 | tf_op jit(solution)/shard_map/while/body/eval_jaxpr/ppermute | solution.py:12
  274.8 11.4 %collective-permute-start = (f32[256,128]{1,0:T(8,128)S(1)}, f32[256,128]{1,0:T(8,128)S(1)}, u32[]{:S(2)}, u32[]{:S(2)}) collective-permute-start(f32[256,128]{1,0:T(8,128)S(1)} %get-tuple-element.432), channel_id=1, source_target_pairs={{127,0},{0,1},{1,2},{2,3},{3,4},{4,5},{5,6},{6,7},{7,8},{8,9},{9,1... | collective-permute-start | bytes 393224 | tf_op jit(solution)/shard_map/while/body/eval_jaxpr/ppermute | solution.py:12
  288.5 11.4 %collective-permute-start = (f32[256,128]{1,0:T(8,128)S(1)}, f32[256,128]{1,0:T(8,128)S(1)}, u32[]{:S(2)}, u32[]{:S(2)}) collective-permute-start(f32[256,128]{1,0:T(8,128)S(1)} %get-tuple-element.432), channel_id=1, source_target_pairs={{127,0},{0,1},{1,2},{2,3},{3,4},{4,5},{5,6},{6,7},{7,8},{8,9},{9,1... | collective-permute-start | bytes 393224 | tf_op jit(solution)/shard_map/while/body/eval_jaxpr/ppermute | solution.py:12
  302.2 11.4 %collective-permute-start = (f32[256,128]{1,0:T(8,128)S(1)}, f32[256,128]{1,0:T(8,128)S(1)}, u32[]{:S(2)}, u32[]{:S(2)}) collective-permute-start(f32[256,128]{1,0:T(8,128)S(1)} %get-tuple-element.432), channel_id=1, source_target_pairs={{127,0},{0,1},{1,2},{2,3},{3,4},{4,5},{5,6},{6,7},{7,8},{8,9},{9,1... | collective-permute-start | bytes 393224 | tf_op jit(solution)/shard_map/while/body/eval_jaxpr/ppermute | solution.py:12
  315.8 11.4 %collective-permute-start = (f32[256,128]{1,0:T(8,128)S(1)}, f32[256,128]{1,0:T(8,128)S(1)}, u32[]{:S(2)}, u32[]{:S(2)}) collective-permute-start(f32[256,128]{1,0:T(8,128)S(1)} %get-tuple-element.432), channel_id=1, source_target_pairs={{127,0},{0,1},{1,2},{2,3},{3,4},{4,5},{5,6},{6,7},{7,8},{8,9},{9,1... | collective-permute-start | bytes 393224 | tf_op jit(solution)/shard_map/while/body/eval_jaxpr/ppermute | solution.py:12
  329.5 11.4 %collective-permute-start = (f32[256,128]{1,0:T(8,128)S(1)}, f32[256,128]{1,0:T(8,128)S(1)}, u32[]{:S(2)}, u32[]{:S(2)}) collective-permute-start(f32[256,128]{1,0:T(8,128)S(1)} %get-tuple-element.432), channel_id=1, source_target_pairs={{127,0},{0,1},{1,2},{2,3},{3,4},{4,5},{5,6},{6,7},{7,8},{8,9},{9,1... | collective-permute-start | bytes 393224 | tf_op jit(solution)/shard_map/while/body/eval_jaxpr/ppermute | solution.py:12
  343.2 11.4 %collective-permute-start = (f32[256,128]{1,0:T(8,128)S(1)}, f32[256,128]{1,0:T(8,128)S(1)}, u32[]{:S(2)}, u32[]{:S(2)}) collective-permute-start(f32[256,128]{1,0:T(8,128)S(1)} %get-tuple-element.432), channel_id=1, source_target_pairs={{127,0},{0,1},{1,2},{2,3},{3,4},{4,5},{5,6},{6,7},{7,8},{8,9},{9,1... | collective-permute-start | bytes 393224 | tf_op jit(solution)/shard_map/while/body/eval_jaxpr/ppermute | solution.py:12
  356.8 11.4 %collective-permute-start = (f32[256,128]{1,0:T(8,128)S(1)}, f32[256,128]{1,0:T(8,128)S(1)}, u32[]{:S(2)}, u32[]{:S(2)}) collective-permute-start(f32[256,128]{1,0:T(8,128)S(1)} %get-tuple-element.432), channel_id=1, source_target_pairs={{127,0},{0,1},{1,2},{2,3},{3,4},{4,5},{5,6},{6,7},{7,8},{8,9},{9,1... | collective-permute-start | bytes 393224 | tf_op jit(solution)/shard_map/while/body/eval_jaxpr/ppermute | solution.py:12
  370.5 11.4 %collective-permute-start = (f32[256,128]{1,0:T(8,128)S(1)}, f32[256,128]{1,0:T(8,128)S(1)}, u32[]{:S(2)}, u32[]{:S(2)}) collective-permute-start(f32[256,128]{1,0:T(8,128)S(1)} %get-tuple-element.432), channel_id=1, source_target_pairs={{127,0},{0,1},{1,2},{2,3},{3,4},{4,5},{5,6},{6,7},{7,8},{8,9},{9,1... | collective-permute-start | bytes 393224 | tf_op jit(solution)/shard_map/while/body/eval_jaxpr/ppermute | solution.py:12
  384.2 11.5 %collective-permute-start = (f32[256,128]{1,0:T(8,128)S(1)}, f32[256,128]{1,0:T(8,128)S(1)}, u32[]{:S(2)}, u32[]{:S(2)}) collective-permute-start(f32[256,128]{1,0:T(8,128)S(1)} %get-tuple-element.432), channel_id=1, source_target_pairs={{127,0},{0,1},{1,2},{2,3},{3,4},{4,5},{5,6},{6,7},{7,8},{8,9},{9,1... | collective-permute-start | bytes 393224 | tf_op jit(solution)/shard_map/while/body/eval_jaxpr/ppermute | solution.py:12
  397.9 12.1 %collective-permute-start = (f32[256,128]{1,0:T(8,128)S(1)}, f32[256,128]{1,0:T(8,128)S(1)}, u32[]{:S(2)}, u32[]{:S(2)}) collective-permute-start(f32[256,128]{1,0:T(8,128)S(1)} %get-tuple-element.432), channel_id=1, source_target_pairs={{127,0},{0,1},{1,2},{2,3},{3,4},{4,5},{5,6},{6,7},{7,8},{8,9},{9,1... | collective-permute-start | bytes 393224 | tf_op jit(solution)/shard_map/while/body/eval_jaxpr/ppermute | solution.py:12
  399.8 11.6 %collective-permute-start.1 = (f32[63,128]{1,0:T(8,128)S(1)}, f32[63,128]{1,0:T(8,128)S(1)}, u32[]{:S(2)}, u32[]{:S(2)}) collective-permute-start(f32[63,128]{1,0:T(8,128)S(1)} %get-tuple-element.434), channel_id=1, source_target_pairs={{127,0},{0,1},{1,2},{2,3},{3,4},{4,5},{5,6},{6,7},{7,8},{8,9},{9,1... | collective-permute-start | bytes 96776 | tf_op jit(solution)/shard_map/while/body/eval_jaxpr/ppermute | solution.py:12
  412.2 13.0 %collective-permute-start = (f32[256,128]{1,0:T(8,128)S(1)}, f32[256,128]{1,0:T(8,128)S(1)}, u32[]{:S(2)}, u32[]{:S(2)}) collective-permute-start(f32[256,128]{1,0:T(8,128)S(1)} %get-tuple-element.432), channel_id=1, source_target_pairs={{127,0},{0,1},{1,2},{2,3},{3,4},{4,5},{5,6},{6,7},{7,8},{8,9},{9,1... | collective-permute-start | bytes 393224 | tf_op jit(solution)/shard_map/while/body/eval_jaxpr/ppermute | solution.py:12
  414.1 12.6 %collective-permute-start.1 = (f32[63,128]{1,0:T(8,128)S(1)}, f32[63,128]{1,0:T(8,128)S(1)}, u32[]{:S(2)}, u32[]{:S(2)}) collective-permute-start(f32[63,128]{1,0:T(8,128)S(1)} %get-tuple-element.434), channel_id=1, source_target_pairs={{127,0},{0,1},{1,2},{2,3},{3,4},{4,5},{5,6},{6,7},{7,8},{8,9},{9,1... | collective-permute-start | bytes 96776 | tf_op jit(solution)/shard_map/while/body/eval_jaxpr/ppermute | solution.py:12
  427.5 12.9 %collective-permute-start = (f32[256,128]{1,0:T(8,128)S(1)}, f32[256,128]{1,0:T(8,128)S(1)}, u32[]{:S(2)}, u32[]{:S(2)}) collective-permute-start(f32[256,128]{1,0:T(8,128)S(1)} %get-tuple-element.432), channel_id=1, source_target_pairs={{127,0},{0,1},{1,2},{2,3},{3,4},{4,5},{5,6},{6,7},{7,8},{8,9},{9,1... | collective-permute-start | bytes 393224 | tf_op jit(solution)/shard_map/while/body/eval_jaxpr/ppermute | solution.py:12
  429.4 12.4 %collective-permute-start.1 = (f32[63,128]{1,0:T(8,128)S(1)}, f32[63,128]{1,0:T(8,128)S(1)}, u32[]{:S(2)}, u32[]{:S(2)}) collective-permute-start(f32[63,128]{1,0:T(8,128)S(1)} %get-tuple-element.434), channel_id=1, source_target_pairs={{127,0},{0,1},{1,2},{2,3},{3,4},{4,5},{5,6},{6,7},{7,8},{8,9},{9,1... | collective-permute-start | bytes 96776 | tf_op jit(solution)/shard_map/while/body/eval_jaxpr/ppermute | solution.py:12
  442.6 11.4 %collective-permute-start = (f32[256,128]{1,0:T(8,128)S(1)}, f32[256,128]{1,0:T(8,128)S(1)}, u32[]{:S(2)}, u32[]{:S(2)}) collective-permute-start(f32[256,128]{1,0:T(8,128)S(1)} %get-tuple-element.432), channel_id=1, source_target_pairs={{127,0},{0,1},{1,2},{2,3},{3,4},{4,5},{5,6},{6,7},{7,8},{8,9},{9,1... | collective-permute-start | bytes 393224 | tf_op jit(solution)/shard_map/while/body/eval_jaxpr/ppermute | solution.py:12
  456.2 11.4 %collective-permute-start = (f32[256,128]{1,0:T(8,128)S(1)}, f32[256,128]{1,0:T(8,128)S(1)}, u32[]{:S(2)}, u32[]{:S(2)}) collective-permute-start(f32[256,128]{1,0:T(8,128)S(1)} %get-tuple-element.432), channel_id=1, source_target_pairs={{127,0},{0,1},{1,2},{2,3},{3,4},{4,5},{5,6},{6,7},{7,8},{8,9},{9,1... | collective-permute-start | bytes 393224 | tf_op jit(solution)/shard_map/while/body/eval_jaxpr/ppermute | solution.py:12
  469.9 11.4 %collective-permute-start = (f32[256,128]{1,0:T(8,128)S(1)}, f32[256,128]{1,0:T(8,128)S(1)}, u32[]{:S(2)}, u32[]{:S(2)}) collective-permute-start(f32[256,128]{1,0:T(8,128)S(1)} %get-tuple-element.432), channel_id=1, source_target_pairs={{127,0},{0,1},{1,2},{2,3},{3,4},{4,5},{5,6},{6,7},{7,8},{8,9},{9,1... | collective-permute-start | bytes 393224 | tf_op jit(solution)/shard_map/while/body/eval_jaxpr/ppermute | solution.py:12
  483.6 11.4 %collective-permute-start = (f32[256,128]{1,0:T(8,128)S(1)}, f32[256,128]{1,0:T(8,128)S(1)}, u32[]{:S(2)}, u32[]{:S(2)}) collective-permute-start(f32[256,128]{1,0:T(8,128)S(1)} %get-tuple-element.432), channel_id=1, source_target_pairs={{127,0},{0,1},{1,2},{2,3},{3,4},{4,5},{5,6},{6,7},{7,8},{8,9},{9,1... | collective-permute-start | bytes 393224 | tf_op jit(solution)/shard_map/while/body/eval_jaxpr/ppermute | solution.py:12
  497.2 11.4 %collective-permute-start = (f32[256,128]{1,0:T(8,128)S(1)}, f32[256,128]{1,0:T(8,128)S(1)}, u32[]{:S(2)}, u32[]{:S(2)}) collective-permute-start(f32[256,128]{1,0:T(8,128)S(1)} %get-tuple-element.432), channel_id=1, source_target_pairs={{127,0},{0,1},{1,2},{2,3},{3,4},{4,5},{5,6},{6,7},{7,8},{8,9},{9,1... | collective-permute-start | bytes 393224 | tf_op jit(solution)/shard_map/while/body/eval_jaxpr/ppermute | solution.py:12
  510.9 11.4 %collective-permute-start = (f32[256,128]{1,0:T(8,128)S(1)}, f32[256,128]{1,0:T(8,128)S(1)}, u32[]{:S(2)}, u32[]{:S(2)}) collective-permute-start(f32[256,128]{1,0:T(8,128)S(1)} %get-tuple-element.432), channel_id=1, source_target_pairs={{127,0},{0,1},{1,2},{2,3},{3,4},{4,5},{5,6},{6,7},{7,8},{8,9},{9,1... | collective-permute-start | bytes 393224 | tf_op jit(solution)/shard_map/while/body/eval_jaxpr/ppermute | solution.py:12
  524.6 11.4 %collective-permute-start = (f32[256,128]{1,0:T(8,128)S(1)}, f32[256,128]{1,0:T(8,128)S(1)}, u32[]{:S(2)}, u32[]{:S(2)}) collective-permute-start(f32[256,128]{1,0:T(8,128)S(1)} %get-tuple-element.432), channel_id=1, source_target_pairs={{127,0},{0,1},{1,2},{2,3},{3,4},{4,5},{5,6},{6,7},{7,8},{8,9},{9,1... | collective-permute-start | bytes 393224 | tf_op jit(solution)/shard_map/while/body/eval_jaxpr/ppermute | solution.py:12
  538.2 11.4 %collective-permute-start = (f32[256,128]{1,0:T(8,128)S(1)}, f32[256,128]{1,0:T(8,128)S(1)}, u32[]{:S(2)}, u32[]{:S(2)}) collective-permute-start(f32[256,128]{1,0:T(8,128)S(1)} %get-tuple-element.432), channel_id=1, source_target_pairs={{127,0},{0,1},{1,2},{2,3},{3,4},{4,5},{5,6},{6,7},{7,8},{8,9},{9,1... | collective-permute-start | bytes 393224 | tf_op jit(solution)/shard_map/while/body/eval_jaxpr/ppermute | solution.py:12
  551.9 11.4 %collective-permute-start = (f32[256,128]{1,0:T(8,128)S(1)}, f32[256,128]{1,0:T(8,128)S(1)}, u32[]{:S(2)}, u32[]{:S(2)}) collective-permute-start(f32[256,128]{1,0:T(8,128)S(1)} %get-tuple-element.432), channel_id=1, source_target_pairs={{127,0},{0,1},{1,2},{2,3},{3,4},{4,5},{5,6},{6,7},{7,8},{8,9},{9,1... | collective-permute-start | bytes 393224 | tf_op jit(solution)/shard_map/while/body/eval_jaxpr/ppermute | solution.py:12
  565.6 11.4 %collective-permute-start = (f32[256,128]{1,0:T(8,128)S(1)}, f32[256,128]{1,0:T(8,128)S(1)}, u32[]{:S(2)}, u32[]{:S(2)}) collective-permute-start(f32[256,128]{1,0:T(8,128)S(1)} %get-tuple-element.432), channel_id=1, source_target_pairs={{127,0},{0,1},{1,2},{2,3},{3,4},{4,5},{5,6},{6,7},{7,8},{8,9},{9,1... | collective-permute-start | bytes 393224 | tf_op jit(solution)/shard_map/while/body/eval_jaxpr/ppermute | solution.py:12
  579.2 11.8 %collective-permute-start = (f32[256,128]{1,0:T(8,128)S(1)}, f32[256,128]{1,0:T(8,128)S(1)}, u32[]{:S(2)}, u32[]{:S(2)}) collective-permute-start(f32[256,128]{1,0:T(8,128)S(1)} %get-tuple-element.432), channel_id=1, source_target_pairs={{127,0},{0,1},{1,2},{2,3},{3,4},{4,5},{5,6},{6,7},{7,8},{8,9},{9,1... | collective-permute-start | bytes 393224 | tf_op jit(solution)/shard_map/while/body/eval_jaxpr/ppermute | solution.py:12
  593.2 12.4 %collective-permute-start = (f32[256,128]{1,0:T(8,128)S(1)}, f32[256,128]{1,0:T(8,128)S(1)}, u32[]{:S(2)}, u32[]{:S(2)}) collective-permute-start(f32[256,128]{1,0:T(8,128)S(1)} %get-tuple-element.432), channel_id=1, source_target_pairs={{127,0},{0,1},{1,2},{2,3},{3,4},{4,5},{5,6},{6,7},{7,8},{8,9},{9,1... | collective-permute-start | bytes 393224 | tf_op jit(solution)/shard_map/while/body/eval_jaxpr/ppermute | solution.py:12
  595.2 12.0 %collective-permute-start.1 = (f32[63,128]{1,0:T(8,128)S(1)}, f32[63,128]{1,0:T(8,128)S(1)}, u32[]{:S(2)}, u32[]{:S(2)}) collective-permute-start(f32[63,128]{1,0:T(8,128)S(1)} %get-tuple-element.434), channel_id=1, source_target_pairs={{127,0},{0,1},{1,2},{2,3},{3,4},{4,5},{5,6},{6,7},{7,8},{8,9},{9,1... | collective-permute-start | bytes 96776 | tf_op jit(solution)/shard_map/while/body/eval_jaxpr/ppermute | solution.py:12
  607.9 13.1 %collective-permute-start = (f32[256,128]{1,0:T(8,128)S(1)}, f32[256,128]{1,0:T(8,128)S(1)}, u32[]{:S(2)}, u32[]{:S(2)}) collective-permute-start(f32[256,128]{1,0:T(8,128)S(1)} %get-tuple-element.432), channel_id=1, source_target_pairs={{127,0},{0,1},{1,2},{2,3},{3,4},{4,5},{5,6},{6,7},{7,8},{8,9},{9,1... | collective-permute-start | bytes 393224 | tf_op jit(solution)/shard_map/while/body/eval_jaxpr/ppermute | solution.py:12
  609.8 12.6 %collective-permute-start.1 = (f32[63,128]{1,0:T(8,128)S(1)}, f32[63,128]{1,0:T(8,128)S(1)}, u32[]{:S(2)}, u32[]{:S(2)}) collective-permute-start(f32[63,128]{1,0:T(8,128)S(1)} %get-tuple-element.434), channel_id=1, source_target_pairs={{127,0},{0,1},{1,2},{2,3},{3,4},{4,5},{5,6},{6,7},{7,8},{8,9},{9,1... | collective-permute-start | bytes 96776 | tf_op jit(solution)/shard_map/while/body/eval_jaxpr/ppermute | solution.py:12
  623.2 12.2 %collective-permute-start = (f32[256,128]{1,0:T(8,128)S(1)}, f32[256,128]{1,0:T(8,128)S(1)}, u32[]{:S(2)}, u32[]{:S(2)}) collective-permute-start(f32[256,128]{1,0:T(8,128)S(1)} %get-tuple-element.432), channel_id=1, source_target_pairs={{127,0},{0,1},{1,2},{2,3},{3,4},{4,5},{5,6},{6,7},{7,8},{8,9},{9,1... | collective-permute-start | bytes 393224 | tf_op jit(solution)/shard_map/while/body/eval_jaxpr/ppermute | solution.py:12
  625.1 11.7 %collective-permute-start.1 = (f32[63,128]{1,0:T(8,128)S(1)}, f32[63,128]{1,0:T(8,128)S(1)}, u32[]{:S(2)}, u32[]{:S(2)}) collective-permute-start(f32[63,128]{1,0:T(8,128)S(1)} %get-tuple-element.434), channel_id=1, source_target_pairs={{127,0},{0,1},{1,2},{2,3},{3,4},{4,5},{5,6},{6,7},{7,8},{8,9},{9,1... | collective-permute-start | bytes 96776 | tf_op jit(solution)/shard_map/while/body/eval_jaxpr/ppermute | solution.py:12
  637.6 11.4 %collective-permute-start = (f32[256,128]{1,0:T(8,128)S(1)}, f32[256,128]{1,0:T(8,128)S(1)}, u32[]{:S(2)}, u32[]{:S(2)}) collective-permute-start(f32[256,128]{1,0:T(8,128)S(1)} %get-tuple-element.432), channel_id=1, source_target_pairs={{127,0},{0,1},{1,2},{2,3},{3,4},{4,5},{5,6},{6,7},{7,8},{8,9},{9,1... | collective-permute-start | bytes 393224 | tf_op jit(solution)/shard_map/while/body/eval_jaxpr/ppermute | solution.py:12
  651.3 11.4 %collective-permute-start = (f32[256,128]{1,0:T(8,128)S(1)}, f32[256,128]{1,0:T(8,128)S(1)}, u32[]{:S(2)}, u32[]{:S(2)}) collective-permute-start(f32[256,128]{1,0:T(8,128)S(1)} %get-tuple-element.432), channel_id=1, source_target_pairs={{127,0},{0,1},{1,2},{2,3},{3,4},{4,5},{5,6},{6,7},{7,8},{8,9},{9,1... | collective-permute-start | bytes 393224 | tf_op jit(solution)/shard_map/while/body/eval_jaxpr/ppermute | solution.py:12
  664.9 11.4 %collective-permute-start = (f32[256,128]{1,0:T(8,128)S(1)}, f32[256,128]{1,0:T(8,128)S(1)}, u32[]{:S(2)}, u32[]{:S(2)}) collective-permute-start(f32[256,128]{1,0:T(8,128)S(1)} %get-tuple-element.432), channel_id=1, source_target_pairs={{127,0},{0,1},{1,2},{2,3},{3,4},{4,5},{5,6},{6,7},{7,8},{8,9},{9,1... | collective-permute-start | bytes 393224 | tf_op jit(solution)/shard_map/while/body/eval_jaxpr/ppermute | solution.py:12
  760.6 11.5 %collective-permute-start = (f32[256,128]{1,0:T(8,128)S(1)}, f32[256,128]{1,0:T(8,128)S(1)}, u32[]{:S(2)}, u32[]{:S(2)}) collective-permute-start(f32[256,128]{1,0:T(8,128)S(1)} %get-tuple-element.432), channel_id=1, source_target_pairs={{127,0},{0,1},{1,2},{2,3},{3,4},{4,5},{5,6},{6,7},{7,8},{8,9},{9,1... | collective-permute-start | bytes 393224 | tf_op jit(solution)/shard_map/while/body/eval_jaxpr/ppermute | solution.py:12
  774.3 12.1 %collective-permute-start = (f32[256,128]{1,0:T(8,128)S(1)}, f32[256,128]{1,0:T(8,128)S(1)}, u32[]{:S(2)}, u32[]{:S(2)}) collective-permute-start(f32[256,128]{1,0:T(8,128)S(1)} %get-tuple-element.432), channel_id=1, source_target_pairs={{127,0},{0,1},{1,2},{2,3},{3,4},{4,5},{5,6},{6,7},{7,8},{8,9},{9,1... | collective-permute-start | bytes 393224 | tf_op jit(solution)/shard_map/while/body/eval_jaxpr/ppermute | solution.py:12
  776.3 11.6 %collective-permute-start.1 = (f32[63,128]{1,0:T(8,128)S(1)}, f32[63,128]{1,0:T(8,128)S(1)}, u32[]{:S(2)}, u32[]{:S(2)}) collective-permute-start(f32[63,128]{1,0:T(8,128)S(1)} %get-tuple-element.434), channel_id=1, source_target_pairs={{127,0},{0,1},{1,2},{2,3},{3,4},{4,5},{5,6},{6,7},{7,8},{8,9},{9,1... | collective-permute-start | bytes 96776 | tf_op jit(solution)/shard_map/while/body/eval_jaxpr/ppermute | solution.py:12
  788.6 13.0 %collective-permute-start = (f32[256,128]{1,0:T(8,128)S(1)}, f32[256,128]{1,0:T(8,128)S(1)}, u32[]{:S(2)}, u32[]{:S(2)}) collective-permute-start(f32[256,128]{1,0:T(8,128)S(1)} %get-tuple-element.432), channel_id=1, source_target_pairs={{127,0},{0,1},{1,2},{2,3},{3,4},{4,5},{5,6},{6,7},{7,8},{8,9},{9,1... | collective-permute-start | bytes 393224 | tf_op jit(solution)/shard_map/while/body/eval_jaxpr/ppermute | solution.py:12
  790.5 12.6 %collective-permute-start.1 = (f32[63,128]{1,0:T(8,128)S(1)}, f32[63,128]{1,0:T(8,128)S(1)}, u32[]{:S(2)}, u32[]{:S(2)}) collective-permute-start(f32[63,128]{1,0:T(8,128)S(1)} %get-tuple-element.434), channel_id=1, source_target_pairs={{127,0},{0,1},{1,2},{2,3},{3,4},{4,5},{5,6},{6,7},{7,8},{8,9},{9,1... | collective-permute-start | bytes 96776 | tf_op jit(solution)/shard_map/while/body/eval_jaxpr/ppermute | solution.py:12
  803.9 12.8 %collective-permute-start = (f32[256,128]{1,0:T(8,128)S(1)}, f32[256,128]{1,0:T(8,128)S(1)}, u32[]{:S(2)}, u32[]{:S(2)}) collective-permute-start(f32[256,128]{1,0:T(8,128)S(1)} %get-tuple-element.432), channel_id=1, source_target_pairs={{127,0},{0,1},{1,2},{2,3},{3,4},{4,5},{5,6},{6,7},{7,8},{8,9},{9,1... | collective-permute-start | bytes 393224 | tf_op jit(solution)/shard_map/while/body/eval_jaxpr/ppermute | solution.py:12
  805.8 12.4 %collective-permute-start.1 = (f32[63,128]{1,0:T(8,128)S(1)}, f32[63,128]{1,0:T(8,128)S(1)}, u32[]{:S(2)}, u32[]{:S(2)}) collective-permute-start(f32[63,128]{1,0:T(8,128)S(1)} %get-tuple-element.434), channel_id=1, source_target_pairs={{127,0},{0,1},{1,2},{2,3},{3,4},{4,5},{5,6},{6,7},{7,8},{8,9},{9,1... | collective-permute-start | bytes 96776 | tf_op jit(solution)/shard_map/while/body/eval_jaxpr/ppermute | solution.py:12
  914.6 11.4 %collective-permute-start = (f32[256,128]{1,0:T(8,128)S(1)}, f32[256,128]{1,0:T(8,128)S(1)}, u32[]{:S(2)}, u32[]{:S(2)}) collective-permute-start(f32[256,128]{1,0:T(8,128)S(1)} %get-tuple-element.432), channel_id=1, source_target_pairs={{127,0},{0,1},{1,2},{2,3},{3,4},{4,5},{5,6},{6,7},{7,8},{8,9},{9,1... | collective-permute-start | bytes 393224 | tf_op jit(solution)/shard_map/while/body/eval_jaxpr/ppermute | solution.py:12
  (72 other events, 735.1 us)
Sparse Core Ops, SparseCore 0:
  953.0 108.5 all-reduce.2
where the time goes:
time: 1080 us; the launch traced here: 1070 us
  waiting for transfers between devices  515 us (48%)
  starting transfers between devices  251 us (23%)
  other arithmetic  196 us (18%)
  matrix products  46.8 us (4%)
  blocking collectives  27.9 us (3%)
  between operations  13.6 us (1%)
  local copies, waits for them, and re-layouts  11.3 us (1%)
    ppermute x129, waiting for transfers between devices, from_behind(): return lax.ppermute(block, axis, route)  407 us
    ppermute x129, starting transfers between devices, from_behind(): return lax.ppermute(block, axis, route)  251 us
    another operation x258, other arithmetic  179 us
    psum x1, waiting for transfers between devices, body(): return lax.psum(total, 'samp') / block_width  109 us
    dot_general x65, matrix products, pair_terms(): lax.dot_general(weighted, panel, (((0,), (0,)), ((), ())), precision=high...  24.4 us
  transfers between devices with their start and end apart: 130, of which 66 were waited for; matrix products, arithmetic and copies ran while one was open for 18% of the time, Pallas kernels for 0%

commit v1 on v0

v1 whole, which is shorter than its diff:
```python
import functools
import math

import jax
import jax.numpy as jnp
from jax import lax
from jax.experimental import pallas as pl
from jax.experimental.pallas import tpu as pltpu
from jax.sharding import PartitionSpec as P

MESH = pl.DeviceIdType.MESH
HIGHEST = lax.Precision.HIGHEST
SIDE = 4
SLOTS = 2 * SIDE + 1
EXTRA = 2 * SIDE


def dot(a, b, contract=((1,), (0,)), precision=None):
    return lax.dot_general(
        a, b, (contract, ((), ())), precision=precision, preferred_element_type=jnp.float32
    )


def split(value):
    high = value.astype(jnp.bfloat16)
    return high, (value - high.astype(jnp.float32)).astype(jnp.bfloat16)


def inverse(matrix, size):
    rows = lax.broadcasted_iota(jnp.int32, (size, size), 0)
    cols = lax.broadcasted_iota(jnp.int32, (size, size), 1)
    for k in range(size):
        row = matrix[k : k + 1, :]
        column = matrix[:, k : k + 1]
        scale = 1.0 / matrix[k : k + 1, k : k + 1]
        left = jnp.where(rows == k, -1.0, column)
        right = jnp.where(cols == k, -1.0, row) * scale
        matrix = jnp.where((rows == k) | (cols == k), 0.0, matrix) - left * right
    return -matrix


def kernel(
    geno, cov, trait, tw_row, tw_col, out,
    gbuf, covb, traitb, pcat, qmat, ysc, hcat, rcat, rfull, tiles, landed, sum_a, sum_b, extra_row,
    send_sem, recv_sem, small_send, small_recv, own_sem, out_send, out_recv,
):
    section = lax.axis_index("samp")
    block = lax.axis_index("var")
    l, k = section // 2, section % 2
    h, z, y = block % 2, (block // 2) % 8, block // 16
    same = (h == l).astype(jnp.int32)
    shift = (1 - l) * (k * (1 - h) + h) + l * (h * k)

    def index(yy, zz, hh):
        return ((yy + 16) % 8 * 8 + (zz + 16) % 8) * 2 + hh

    def side_block(slot):
        if slot < SIDE:
            return index(y, z + shift + slot, h)
        if slot < EXTRA:
            return index(y + 4 * k + slot - SIDE, z, l)
        return index(y, z + 4 * (1 - k), h)

    def is_me(samp, var):
        return (samp == section) & (var == block)

    users = []
    for i in range(2):
        for kk in range(2):
            first = kk * (1 - h) + h if i == 0 else h * kk
            for a in range(SIDE):
                users.append((a, 2 * i + kk, index(y, z - first - a, h)))
    for j in range(2):
        for kk in range(2):
            for b in range(SIDE):
                users.append((SIDE + b, 2 * h + kk, index(y - 4 * kk - b, z, j)))
    users.append((EXTRA, 2 * h, index(y, z + 4, h)))
    users.append((EXTRA, 2 * h + 1, block))

    own_cov = pltpu.make_async_copy(cov, covb.at[section], own_sem.at[0])
    own_trait = pltpu.make_async_copy(trait, traitb.at[section], own_sem.at[1])
    own_cov.start()
    own_trait.start()

    barrier = pltpu.get_barrier_semaphore()
    for step in range(1, 4):
        pl.semaphore_signal(barrier, inc=1, device_id=((section + step) % 4, block), device_id_type=MESH)
    for slot in range(SLOTS):
        owner = side_block(slot)
        for q in range(4):
            wanted = jnp.logical_not(is_me(q, owner))
            if slot == EXTRA:
                wanted = wanted & (same == 1)

            @pl.when(wanted)
            def _():
                pl.semaphore_signal(barrier, inc=1, device_id=(q, owner), device_id_type=MESH)

    selves = same + (shift == 0).astype(jnp.int32)
    pl.semaphore_wait(barrier, len(users) + 3 - selves)

    small = []
    for step in range(1, 4):
        peer = ((section + step) % 4, block)
        for n, (src, dst) in enumerate(((cov, covb), (trait, traitb))):
            small.append(
                pltpu.make_async_remote_copy(
                    src_ref=src, dst_ref=dst.at[section], send_sem=small_send.at[n, step - 1],
                    recv_sem=small_recv.at[n, 3 - step], device_id=peer, device_id_type=MESH,
                )
            )
    for copy in small:
        copy.start()

    remotes = []
    for n, (slot, samp, var) in enumerate(users):
        mine = is_me(samp, var)
        remote = pltpu.make_async_remote_copy(
            src_ref=geno, dst_ref=gbuf.at[slot, section], send_sem=send_sem.at[n],
            recv_sem=recv_sem.at[slot], device_id=(samp, var), device_id_type=MESH,
        )
        remotes.append((mine, remote))
        pl.when(jnp.logical_not(mine))(remote.start)
        pl.when(mine)(pltpu.make_async_copy(geno, gbuf.at[slot, section], recv_sem.at[slot]).start)

    own_cov.wait()
    own_trait.wait()
    for copy in small:
        copy.wait()

    count, width = covb.shape[0] * covb.shape[1], covb.shape[2]
    covs = covb[...].reshape(count, width)
    traits = traitb[...].reshape(count, traitb.shape[2])
    eye = (
        lax.broadcasted_iota(jnp.int32, (width, width), 0)
        == lax.broadcasted_iota(jnp.int32, (width, width), 1)
    ).astype(jnp.float32)
    cross = dot(covs, covs, ((0,), (0,)), HIGHEST) + count / 10.0 * eye
    solved = dot(covs, inverse(cross, width), precision=HIGHEST)
    hat = dot(solved, covs, ((1,), (1,)), HIGHEST)
    diagonal = lax.broadcasted_iota(jnp.int32, (count, count), 0) == lax.broadcasted_iota(
        jnp.int32, (count, count), 1
    )
    project = jnp.where(diagonal, 1.0, 0.0) - hat
    high, low = split(project)
    pcat[:, :count] = high
    pcat[:, count:] = low
    scaled = dot(project, traits, precision=HIGHEST) * (1.0 / math.sqrt(count))
    ysc[...] = scaled
    qmat[...] = dot(scaled * tw_row[...], scaled, ((1,), (1,)), HIGHEST)

    def arrive(slot):
        pltpu.make_async_copy(gbuf.at[slot], gbuf.at[slot], recv_sem.at[slot]).wait()
        centred = (gbuf[slot].astype(jnp.float32) - 1.0).astype(jnp.bfloat16)
        centred = centred.reshape(count, centred.shape[-1])
        return dot(pcat[...], jnp.concatenate([centred, centred], axis=0))

    def make_h(slot, high, low):
        wide = jnp.concatenate([high, low], axis=1)
        twice = jnp.concatenate([high, high], axis=1)
        gram = dot(wide, twice, ((1,), (1,))) + dot(high, low, ((1,), (1,)))
        h_high, h_low = split(gram * qmat[...])
        rows = pl.ds(pl.multiple_of(slot * count, count), count)
        hcat[rows, :count] = h_high
        hcat[rows, count : 2 * count] = h_high
        hcat[rows, 2 * count :] = h_low

    def prepare(slot, carry):
        resid = arrive(slot)
        high, low = split(resid)
        side, at = slot // SIDE, pl.ds(pl.multiple_of(slot % SIDE * 128, 128), 128)
        rfull[side, :, at] = resid
        rcat[side, :count, at] = high
        rcat[side, count : 2 * count, at] = low
        rcat[side, 2 * count :, at] = high
        make_h(slot, high, low)
        return carry

    lax.fori_loop(0, EXTRA, prepare, 0)

    def score(step, carry):
        side, part = step // 2, step % 2
        at = pl.ds(pl.multiple_of(part * 256, 256), 256)
        rows = pl.ds(pl.multiple_of((1 - side) * SIDE * count, SIDE * count), SIDE * count)
        product = dot(hcat[rows, :], rcat[side, :, at])
        weighted = product.reshape(SIDE, count, 256) * rfull[side, :, at][None]
        sums = jnp.sum(weighted, axis=1)
        sums = jnp.concatenate([sums, jnp.zeros_like(sums)], axis=0)
        sums = pltpu.roll(sums, jnp.where(side == 0, 4 * k, shift), 0)
        first = side * SIDE + part * 2
        tiles[first] = sums[:, :128]
        tiles[first + 1] = sums[:, 128:]
        return carry

    lax.fori_loop(0, 4, score, 0)

    row_ids = lax.broadcasted_iota(jnp.int32, (8, 128), 0)

    @pl.when(same == 1)
    def _():
        high, low = split(arrive(EXTRA))
        make_h(EXTRA, high, low)
        product = dot(hcat[EXTRA * count :, :], rcat[1, :, :128])
        extra = jnp.sum(product * rfull[1, :, :128], axis=0, keepdims=True)
        tile = jnp.where(row_ids == 4 * k, 0.0, tiles[SIDE])
        tiles[SIDE] = jnp.where(row_ids == 4 * (1 - k), extra, tile)

    @pl.when((same == 1) & (k == 0))
    def _():
        resid = rfull[0, :, :128]
        own = dot(ysc[...], resid * resid, ((0,), (0,)), HIGHEST)
        own = jnp.sum(own * own * tw_col[...], axis=0, keepdims=True)
        tiles[0] = tiles[0] - jnp.where(row_ids == 0, own, 0.0)

    returns = []
    for slot in range(EXTRA):
        owner = side_block(slot)
        at = l * 8 + k * 4 + slot if slot < SIDE else 16 + h * 8 + k * 4 + slot - SIDE
        for q in range(4):
            mine = is_me(q, owner)
            remote = pltpu.make_async_remote_copy(
                src_ref=tiles.at[slot], dst_ref=landed.at[at], send_sem=out_send.at[slot * 4 + q],
                recv_sem=out_recv, device_id=(q, owner), device_id_type=MESH,
            )
            returns.append((mine, remote))
            pl.when(jnp.logical_not(mine))(remote.start)
            pl.when(mine)(pltpu.make_async_copy(tiles.at[slot], landed.at[at], out_recv).start)

    sum_a[...] = jnp.zeros_like(sum_a)
    for mine, remote in remotes + returns:
        pl.when(jnp.logical_not(mine))(remote.wait_send)
    pltpu.make_async_copy(landed, landed, out_recv).wait()

    for i in range(2):
        for kk in range(2):
            first = kk * (1 - h) + h if i == 0 else h * kk
            for n in range(SIDE):
                at = i * 8 + kk * 4 + n
                there = pl.ds((z + 8 - first - n) % 8 * 2 + i, 8, stride=16)
                sum_a[there, :] = sum_a[there, :] + pltpu.roll(landed[at], y, 0)
                there = pl.ds((y + 8 - 4 * kk - n) % 8 * 16 + i, 8, stride=2)
                sum_b[there, :] = pltpu.roll(landed[16 + at], z, 0)
    out[...] = (sum_a[...] + sum_b[...]).T * (1.0 / out.shape[0])


def body(genotypes, covariates, traits, trait_weights):
    part, width = genotypes.shape
    count = 4 * part
    cov_count, trait_count = covariates.shape[1], traits.shape[1]
    f32, bf16 = jnp.float32, jnp.bfloat16
    anywhere = pl.BlockSpec(memory_space=pl.ANY)
    vmem = pl.BlockSpec(memory_space=pltpu.VMEM)
    dma = pltpu.SemaphoreType.DMA
    return pl.pallas_call(
        kernel,
        name="epistasis",
        out_shape=jax.ShapeDtypeStruct((width, 128), f32),
        in_specs=[anywhere, anywhere, anywhere, vmem, vmem],
        out_specs=vmem,
        scratch_shapes=[
            pltpu.VMEM((SLOTS, 4, part, width), jnp.int32),
            pltpu.VMEM((4, part, cov_count), f32),
            pltpu.VMEM((4, part, trait_count), f32),
            pltpu.VMEM((count, 2 * count), bf16),
            pltpu.VMEM((count, count), f32),
            pltpu.VMEM((count, trait_count), f32),
            pltpu.VMEM((SLOTS * count, 3 * count), bf16),
            pltpu.VMEM((2, 3 * count, SIDE * width), bf16),
            pltpu.VMEM((2, count, SIDE * width), f32),
            pltpu.VMEM((EXTRA, 8, width), f32),
            pltpu.VMEM((32, 8, width), f32),
            pltpu.VMEM((128, width), f32),
            pltpu.VMEM((128, width), f32),
            pltpu.VMEM((8, width), f32),
            dma((34,)), dma((SLOTS,)), dma((2, 3)), dma((2, 3)), dma((2,)), dma((32,)), dma,
        ],
        compiler_params=pltpu.CompilerParams(
            collective_id=0, has_side_effects=True, vmem_limit_bytes=48 << 20
        ),
    )(genotypes, covariates, traits, trait_weights[None, :], trait_weights[:, None])


def solution(mesh):
    placed = (P("samp", "var"), P("samp", None), P("samp", None), P())
    return jax.shard_map(
        body, mesh=mesh, in_specs=placed, out_specs=P("var", None), check_vma=False
    )
```

time: 1080 us -> 54 us (0.05)
  the two profiles are of different devices: /device:TPU:1 before, /device:TPU:5 now
where the time goes in v1:
time: 54 us; the launch traced here: 53.8 us
  Pallas kernels  51.5 us (95%)
  local copies, waits for them, and re-layouts  2.28 us (4%)
    pallas_call x1, Pallas kernels, body(): pl.pallas_call(kernel, name='epistasis', out_shape=jax.ShapeDtypeStruct((...  51.5 us
    unnamed x9, local copies, waits for them, and re-layouts  2.2 us

profile of v1, /device:TPU:5, one launch (start us, length us, event | category | flops | bytes accessed | tf_op | source)
XLA Modules:
  0.0 53.8 jit_solution(8487863931107799920)
XLA Ops:
  0.0 0.0 copy-start.1
  0.0 0.7 %copy-done.1 = f32[8]{0:T(128)S(1)} copy-done((f32[8]{0:T(128)S(1)}, f32[8]{0:T(128)}, u32[]{:S(2)}) %copy-start.1) | copy-done | bytes 56
  0.7 0.1 copy.7.tw_col
  0.7 0.0 copy-start.2
  0.7 0.0 copy-start
  0.7 0.8 %copy.5.cov = f32[64,40]{1,0:T(8,128)S(1)} copy(f32[64,40]{0,1:T(8,128)} %param.5) | data formatting | bytes 20480 | tf_op args[1]
  1.6 0.0 copy-done.2
  1.6 0.1 copy.6.trait
  1.7 0.0 copy-done
  1.7 51.5 %epistasis.1 = f32[128,128]{1,0:T(8,128)S(1)} custom-call(s32[64,128]{1,0:T(8,128)S(1)} %copy-done, f32[64,40]{1,0:T(8,128)S(1)} %copy.5.cov, f32[64,8]{1,0:T(8,128)S(1)} %copy.6.trait, f32[1,8]{1,0:T(1,128)S(1)} %bitcast.3, f32[8,1]{1,0:T(8,128)S(1)} %copy.7.tw_col), custom_call_target="tpu_custom_call" | custom-call | tf_op jit(solution)/shard_map/epistasis/pallas_call | solution.py:254
  53.2 0.6 %copy.9 = f32[128,128]{1,0:T(8,128)} copy(f32[128,128]{1,0:T(8,128)S(1)} %epistasis.1) | data formatting | bytes 131072
Async XLA Ops:
  0.0 0.7 %copy-start.1 = (f32[8]{0:T(128)S(1)}, f32[8]{0:T(128)}, u32[]{:S(2)}) copy-start(f32[8]{0:T(128)} %param.7) | copy-start | bytes 100
  0.7 0.8 %copy-start.2 = (f32[64,8]{0,1:T(8,128)S(1)}, f32[64,8]{0,1:T(8,128)}, u32[]{:S(2)}) copy-start(f32[64,8]{0,1:T(8,128)} %param.6) | copy-start | bytes 6148
  0.7 0.9 %copy-start = (s32[64,128]{1,0:T(8,128)S(1)}, s32[64,128]{1,0:T(8,128)}, u32[]{:S(2)}) copy-start(s32[64,128]{1,0:T(8,128)} %geno.1) | copy-start | bytes 98308

commit v2 on v1

v2 whole, which is shorter than its diff:
```python
import math

import jax
import jax.numpy as jnp
from jax import lax
from jax.experimental import pallas as pl
from jax.experimental.pallas import tpu as pltpu
from jax.sharding import PartitionSpec as P

MESH = pl.DeviceIdType.MESH
HIGHEST = lax.Precision.HIGHEST
SIDE = 4
ALONG_Z = (0, 1, 2, -3, 4)
A_SLOTS = len(ALONG_Z)


def dot(a, b, contract=((1,), (0,)), precision=None):
    return lax.dot_general(
        a, b, (contract, ((), ())), precision=precision, preferred_element_type=jnp.float32
    )


def split(value):
    high = value.astype(jnp.bfloat16)
    return high, (value - high.astype(jnp.float32)).astype(jnp.bfloat16)


def sweep(matrix, begin, end):
    size = matrix.shape[0]
    rows = lax.broadcasted_iota(jnp.int32, (size, size), 0)
    cols = lax.broadcasted_iota(jnp.int32, (size, size), 1)
    for k in range(begin, end, 2):
        row_1, row_2 = matrix[k : k + 1, :], matrix[k + 1 : k + 2, :]
        col_1, col_2 = matrix[:, k : k + 1], matrix[:, k + 1 : k + 2]
        p, q, r = row_1[:, k : k + 1], row_1[:, k + 1 : k + 2], row_2[:, k + 1 : k + 2]
        scale = 1.0 / (p * r - q * q)
        row_1 = jnp.where(cols == k, -1.0, jnp.where(cols == k + 1, 0.0, row_1))
        row_2 = jnp.where(cols == k + 1, -1.0, jnp.where(cols == k, 0.0, row_2))
        col_1 = jnp.where(rows == k, -1.0, jnp.where(rows == k + 1, 0.0, col_1))
        col_2 = jnp.where(rows == k + 1, -1.0, jnp.where(rows == k, 0.0, col_2))
        kept = (rows == k) | (rows == k + 1) | (cols == k) | (cols == k + 1)
        matrix = (
            jnp.where(kept, 0.0, matrix)
            - col_1 * ((r * row_1 - q * row_2) * scale)
            - col_2 * ((p * row_2 - q * row_1) * scale)
        )
    return matrix


def kernel(
    geno, cov, trait, weights, out,
    line, abuf, bbuf, covb, traitb, tw, pcat, qmat, ysc, hcat, rcat_a, rcat_b, rfull_a, rfull_b,
    tiles, landed, sum_a, sum_b,
    z_send, z_recv, y_send, y_recv, bx_send, bx_recv, ax_send, ax_recv, core_send, core_recv,
    small_send, small_recv, own_sem, out_send, out_recv,
):
    section = lax.axis_index("samp")
    block = lax.axis_index("var")
    l, k = section // 2, section % 2
    h, z, y = block % 2, (block // 2) % 8, block // 16
    same = (h == l).astype(jnp.int32)
    shift = same * k + (1 - same) * h

    def index(yy, zz, hh):
        return ((yy + 16) % 8 * 8 + (zz + 16) % 8) * 2 + hh

    def samp(ll, kk):
        return 2 * ll + kk

    def is_me(target):
        return (target[0] == section) & (target[1] == block)

    def unless_me(target, action):
        pl.when(jnp.logical_not(is_me(target)))(action)

    def send(src, dst, send_sem, recv_sem, target):
        return pltpu.make_async_remote_copy(
            src_ref=src, dst_ref=dst, send_sem=send_sem, recv_sem=recv_sem,
            device_id=target, device_id_type=MESH,
        )

    def send_or_copy(src, dst, send_sem, recv_sem, target):
        mine = is_me(target)
        remote = send(src, dst, send_sem, recv_sem, target)
        pl.when(jnp.logical_not(mine))(remote.start)
        pl.when(mine)(pltpu.make_async_copy(src, dst, recv_sem).start)
        return lambda: unless_me(target, remote.wait_send)

    def landing(ref, sem):
        pltpu.make_async_copy(ref, ref, sem).wait()

    own = [
        pltpu.make_async_copy(cov, covb.at[2 * k + l], own_sem.at[0]),
        pltpu.make_async_copy(trait, traitb.at[2 * k + l], own_sem.at[1]),
        pltpu.make_async_copy(weights, tw, own_sem.at[2]),
    ]
    for copy in own:
        copy.start()

    peers = [((section + step) % 4, block) for step in range(1, 4)]
    z_targets = [(section, index(y, z - d, h)) for d in ALONG_Z[1:]]
    z_sources = [(section, index(y, z + d, h)) for d in ALONG_Z[1:]]
    y_targets = [(samp(l, e // SIDE), index(y - e, z, h)) for e in range(8)]
    y_sources = [
        (samp(l, kk), index(y + 4 * k + b, z, h)) for b in range(SIDE) for kk in range(2)
    ]
    beside = (samp(1 - l, k), block)
    sibling = (samp(l, 1 - k), block)
    ax_targets = [(samp(h, k), index(y, z, hh)) for hh in range(2)]
    ax_sources = [(samp(ll, k), index(y, z, l)) for ll in range(2)]

    barrier = pltpu.get_barrier_semaphore()
    for source in peers + z_sources + y_sources + [beside, sibling] + ax_sources:
        unless_me(
            source,
            lambda source=source: pl.semaphore_signal(
                barrier, inc=1, device_id=source, device_id_type=MESH
            ),
        )
    pl.semaphore_wait(barrier, 19 - (1 - k) - same)

    sent = []
    small = []
    for n, peer in enumerate(peers):
        for m, (src, dst) in enumerate(((cov, covb), (trait, traitb))):
            copy = send(src, dst.at[2 * k + l], small_send.at[m, n], small_recv.at[m, 2 - n], peer)
            copy.start()
            small.append(copy)
    for n in reversed(range(4)):
        copy = send(geno, line.at[n], z_send.at[n], z_recv.at[n], z_targets[n])
        copy.start()
        sent.append(copy.wait_send)
    for e in (4, 3, 5, 2, 6, 1, 7, 0):
        dst = bbuf.at[e % SIDE, k, l]
        sent.append(send_or_copy(geno, dst, y_send.at[e], y_recv.at[e % SIDE], y_targets[e]))

    def pass_a(slot):
        src = geno if slot == 0 else line.at[slot - 1]
        if slot > 0:
            landing(src, z_recv.at[slot - 1])
        for n, target in enumerate(ax_targets):
            dst = abuf.at[slot, k, l]
            sent.append(send_or_copy(src, dst, ax_send.at[slot, n], ax_recv.at[slot], target))

    def pass_b(step):
        slot = step + k * (SIDE - 1 - 2 * step)
        half = bbuf.at[slot, :, l]
        landing(half, y_recv.at[slot])
        copy = send(half, half, bx_send.at[step], bx_recv.at[slot], beside)
        copy.start()
        sent.append(copy.wait_send)

    def pass_core(slot):
        part = abuf.at[slot, k]
        landing(part, ax_recv.at[slot])
        copy = send(part, part, core_send.at[slot], core_recv.at[slot], sibling)
        copy.start()
        sent.append(copy.wait_send)

    pass_a(0)
    for copy in own + small:
        copy.wait()
    cov_t = jnp.concatenate([covb[n] for n in range(4)], axis=1)
    trait_t = jnp.concatenate([traitb[n] for n in range(4)], axis=1)
    width, count = cov_t.shape
    eye = (
        lax.broadcasted_iota(jnp.int32, (width, width), 0)
        == lax.broadcasted_iota(jnp.int32, (width, width), 1)
    ).astype(jnp.float32)
    swept = dot(cov_t, cov_t, ((1,), (1,)), HIGHEST) + count / 10.0 * eye
    pass_a(1)
    pass_b(0)
    swept = sweep(swept, 0, width // 4)
    pass_b(1)
    swept = sweep(swept, width // 4, width // 2)
    pass_a(2)
    pass_core(0)
    swept = sweep(swept, width // 2, width * 3 // 4)
    pass_a(3)
    pass_b(2)
    swept = sweep(swept, width * 3 // 4, width)
    pass_core(1)
    solved = dot(-swept, cov_t, precision=HIGHEST)
    hat = dot(cov_t, solved, ((0,), (0,)), HIGHEST)
    diagonal = lax.broadcasted_iota(jnp.int32, (count, count), 0) == lax.broadcasted_iota(
        jnp.int32, (count, count), 1
    )
    project = jnp.where(diagonal, 1.0, 0.0) - hat
    high, low = split(project)
    pcat[:, :count] = high
    pcat[:, count:] = low
    pass_b(3)
    pass_a(4)
    pass_core(2)
    scaled = dot(trait_t, project, precision=HIGHEST) * (1.0 / math.sqrt(count))
    ysc[...] = scaled
    traits_id = lax.broadcasted_iota(jnp.int32, (scaled.shape[0], 1), 0)
    tw_col = sum(jnp.where(traits_id == t, tw[t], 0.0) for t in range(scaled.shape[0]))
    qmat[...] = dot(scaled * tw_col, scaled, ((0,), (0,)), HIGHEST)
    pass_core(3)
    pass_core(4)

    def prepare(genotypes, at, rcat, rfull, hrow):
        centred = (genotypes.astype(jnp.float32) - 1.0).astype(jnp.bfloat16).reshape(count, 128)
        resid = dot(pcat[...], jnp.concatenate([centred, centred], axis=0))
        high, low = split(resid)
        at = pl.ds(pl.multiple_of(at * 128, 128), 128)
        rfull[:, at] = resid
        rcat[:count, at] = high
        rcat[count : 2 * count, at] = low
        rcat[2 * count :, at] = high
        wide = jnp.concatenate([high, low], axis=1)
        twice = jnp.concatenate([high, high], axis=1)
        gram = dot(wide, twice, ((1,), (1,))) + dot(high, low, ((1,), (1,)))
        h_high, h_low = split(gram * qmat[...])
        rows = pl.ds(pl.multiple_of(hrow * count, count), count)
        hcat[rows, :count] = h_high
        hcat[rows, count : 2 * count] = h_high
        hcat[rows, 2 * count :] = h_low

    def prepare_b(step, carry):
        slot = step + k * (SIDE - 1 - 2 * step)
        landing(bbuf.at[slot, :, 1 - l], bx_recv.at[slot])
        prepare(bbuf[slot], slot, rcat_b, rfull_b, A_SLOTS + slot)
        return carry

    def prepare_a(slot, carry):
        landing(abuf.at[slot, 1 - k], core_recv.at[slot])
        prepare(abuf[slot], slot, rcat_a, rfull_a, slot)
        return carry

    lax.fori_loop(0, SIDE, prepare_b, 0)
    lax.fori_loop(0, A_SLOTS, prepare_a, 0)

    def pairs(hrow, rcat, rfull, at):
        at = pl.ds(pl.multiple_of(at * 128, 128), 256)
        rows = pl.ds(pl.multiple_of(hrow * count, count), SIDE * count)
        product = dot(hcat[rows, :], rcat[:, at])
        weighted = product.reshape(SIDE, count, 256) * rfull[:, at][None]
        sums = jnp.sum(weighted, axis=1)
        return jnp.concatenate([sums, jnp.zeros_like(sums)], axis=0)

    def score_a(part, carry):
        sums = pairs(A_SLOTS, rcat_a, rfull_a, shift + 2 * part)
        sums = pltpu.roll(sums, 4 * k, 0)
        tiles[2 * part] = sums[:, :128]
        tiles[2 * part + 1] = sums[:, 128:]
        return carry

    def by_offset(sums):
        sums = pltpu.roll(sums, shift, 0)
        picked = [sums[a : a + 1] for a in (0, 1, 2, 5, 4, 3, 6, 7)]
        return jnp.concatenate(picked, axis=0)

    def score_b(part, carry):
        sums = by_offset(pairs(shift, rcat_b, rfull_b, 2 * part))
        tiles[SIDE + 2 * part] = sums[:, :128]
        tiles[SIDE + 2 * part + 1] = sums[:, 128:]
        return carry

    lax.fori_loop(0, 2, score_b, 0)
    lax.fori_loop(0, 2, score_a, 0)

    row_ids = lax.broadcasted_iota(jnp.int32, (8, 128), 0)

    @pl.when(same == 1)
    def _():
        rows = pl.ds(pl.multiple_of((1 - k) * 4 * count, count), count)
        product = dot(hcat[rows, :], rcat_b[:, :128])
        extra = jnp.sum(product * rfull_b[:, :128], axis=0, keepdims=True)
        tile = jnp.where(row_ids == 4 * k, 0.0, tiles[SIDE])
        tiles[SIDE] = jnp.where(row_ids == 4 * (1 - k), extra, tile)

    @pl.when((same == 1) & (k == 0))
    def _():
        resid = rfull_a[:, :128]
        diag = dot(ysc[...], resid * resid, precision=HIGHEST)
        diag = jnp.sum(diag * diag * tw_col, axis=0, keepdims=True)
        tiles[0] = tiles[0] - jnp.where(row_ids == 0, diag, 0.0)

    for slot in range(2 * SIDE):
        if slot < SIDE:
            offset = jnp.where(shift == 0, ALONG_Z[slot], ALONG_Z[slot + 1])
            owner, at = index(y, z + offset, l), h * 8 + k * 4 + slot
        else:
            owner, at = index(y + 4 * k + slot - SIDE, z, h), 16 + l * 8 + k * 4 + slot - SIDE
        for q in range(4):
            sent.append(
                send_or_copy(
                    tiles.at[slot], landed.at[at], out_send.at[slot * 4 + q], out_recv, (q, owner)
                )
            )

    sum_a[...] = jnp.zeros_like(sum_a)
    for wait in sent:
        wait()
    landing(landed, out_recv)

    for i in range(2):
        mixed = jnp.not_equal(h, i).astype(jnp.int32)
        for kk in range(2):
            first = mixed * (1 - h) + (1 - mixed) * kk
            for n in range(SIDE):
                at = i * 8 + kk * 4 + n
                offset = jnp.where(first == 0, ALONG_Z[n], ALONG_Z[n + 1])
                there = pl.ds((z + 8 - offset) % 8 * 2 + i, 8, stride=16)
                sum_a[there, :] = sum_a[there, :] + pltpu.roll(landed[at], y, 0)
                there = pl.ds((y + 8 - 4 * kk - n) % 8 * 16 + i, 8, stride=2)
                sum_b[there, :] = pltpu.roll(landed[16 + at], z, 0)
    out[...] = (sum_a[...] + sum_b[...]).T * (1.0 / out.shape[0])


def body(genotypes, covariates, traits, trait_weights):
    part, width = genotypes.shape
    count = 4 * part
    cov_count, trait_count = covariates.shape[1], traits.shape[1]
    f32, bf16, i32 = jnp.float32, jnp.bfloat16, jnp.int32
    dma = pltpu.SemaphoreType.DMA
    return pl.pallas_call(
        kernel,
        name="epistasis",
        out_shape=jax.ShapeDtypeStruct((width, 128), f32),
        in_specs=[pl.BlockSpec(memory_space=pl.ANY)] * 4,
        out_specs=pl.BlockSpec(memory_space=pltpu.VMEM),
        scratch_shapes=[
            pltpu.VMEM((A_SLOTS - 1, part, width), i32),
            pltpu.VMEM((A_SLOTS, 2, 2, part, width), i32),
            pltpu.VMEM((SIDE, 2, 2, part, width), i32),
            pltpu.VMEM((4, cov_count, part), f32),
            pltpu.VMEM((4, trait_count, part), f32),
            pltpu.SMEM((trait_count,), f32),
            pltpu.VMEM((count, 2 * count), bf16),
            pltpu.VMEM((count, count), f32),
            pltpu.VMEM((trait_count, count), f32),
            pltpu.VMEM(((A_SLOTS + SIDE) * count, 3 * count), bf16),
            pltpu.VMEM((3 * count, A_SLOTS * width), bf16),
            pltpu.VMEM((3 * count, SIDE * width), bf16),
            pltpu.VMEM((count, A_SLOTS * width), f32),
            pltpu.VMEM((count, SIDE * width), f32),
            pltpu.VMEM((2 * SIDE, 8, width), f32),
            pltpu.VMEM((32, 8, width), f32),
            pltpu.VMEM((128, width), f32),
            pltpu.VMEM((128, width), f32),
            dma((4,)), dma((4,)), dma((8,)), dma((SIDE,)), dma((SIDE,)), dma((SIDE,)),
            dma((A_SLOTS, 2)), dma((A_SLOTS,)), dma((A_SLOTS,)), dma((A_SLOTS,)),
            dma((2, 3)), dma((2, 3)), dma((3,)), dma((32,)), dma,
        ],
        compiler_params=pltpu.CompilerParams(
            collective_id=0, has_side_effects=True, vmem_limit_bytes=56 << 20
        ),
    )(genotypes, covariates.T, traits.T, trait_weights)


def solution(mesh):
    placed = (P("samp", "var"), P("samp", None), P("samp", None), P())
    return jax.shard_map(
        body, mesh=mesh, in_specs=placed, out_specs=P("var", None), check_vma=False
    )
```

time: 54 us -> 47.5 us (0.88)
  the two profiles are of different devices: /device:TPU:5 before, /device:TPU:1 now
where the time goes in v2:
time: 47.5 us; the launch traced here: 47.4 us
  Pallas kernels  45.9 us (97%)
  local copies, waits for them, and re-layouts  1.47 us (3%)
    pallas_call x1, Pallas kernels, body(): pl.pallas_call(kernel, name='epistasis', out_shape=jax.ShapeDtypeStruct((...  45.9 us
    unnamed x1, local copies, waits for them, and re-layouts  1.47 us

profile of v2, /device:TPU:1, one launch (start us, length us, event | category | flops | bytes accessed | tf_op | source)
XLA Modules:
  0.0 47.4 jit_solution(7948356412659258352)
XLA Ops:
  0.0 45.9 %epistasis.1 = f32[128,128]{1,0:T(8,128)} custom-call(s32[64,128]{1,0:T(8,128)} %geno.1, f32[40,64]{1,0:T(8,128)} %bitcast.2, f32[8,64]{1,0:T(8,128)} %bitcast.3, f32[8]{0:T(128)} %weights.1), custom_call_target="tpu_custom_call" | custom-call | tf_op jit(solution)/shard_map/epistasis/pallas_call | solution.py:319
  45.9 1.5 %copy.6 = f32[128,128]{1,0:T(8,128)} copy(f32[128,128]{1,0:T(8,128)} %epistasis.1) | data formatting | bytes 131072

commit v3 on v2

v3 whole, which is shorter than its diff:
```python
import math

import jax
import jax.numpy as jnp
from jax import lax
from jax.experimental import pallas as pl
from jax.experimental.pallas import tpu as pltpu
from jax.sharding import PartitionSpec as P

MESH = pl.DeviceIdType.MESH
HIGHEST = lax.Precision.HIGHEST
SIDE = 4
ALONG_Z = (0, 1, 2, -3, 4)
A_SLOTS = len(ALONG_Z)


def dot(a, b, contract=((1,), (0,)), precision=None):
    return lax.dot_general(
        a, b, (contract, ((), ())), precision=precision, preferred_element_type=jnp.float32
    )


def split(value):
    high = value.astype(jnp.bfloat16)
    return high, (value - high.astype(jnp.float32)).astype(jnp.bfloat16)


def sweep(matrix, begin, end):
    size = matrix.shape[0]
    rows = lax.broadcasted_iota(jnp.int32, (size, size), 0)
    cols = lax.broadcasted_iota(jnp.int32, (size, size), 1)
    for k in range(begin, end, 2):
        row_1, row_2 = matrix[k : k + 1, :], matrix[k + 1 : k + 2, :]
        col_1, col_2 = matrix[:, k : k + 1], matrix[:, k + 1 : k + 2]
        p, q, r = row_1[:, k : k + 1], row_1[:, k + 1 : k + 2], row_2[:, k + 1 : k + 2]
        scale = 1.0 / (p * r - q * q)
        row_1 = jnp.where(cols == k, -1.0, jnp.where(cols == k + 1, 0.0, row_1))
        row_2 = jnp.where(cols == k + 1, -1.0, jnp.where(cols == k, 0.0, row_2))
        col_1 = jnp.where(rows == k, -1.0, jnp.where(rows == k + 1, 0.0, col_1))
        col_2 = jnp.where(rows == k + 1, -1.0, jnp.where(rows == k, 0.0, col_2))
        kept = (rows == k) | (rows == k + 1) | (cols == k) | (cols == k + 1)
        matrix = (
            jnp.where(kept, 0.0, matrix)
            - col_1 * ((r * row_1 - q * row_2) * scale)
            - col_2 * ((p * row_2 - q * row_1) * scale)
        )
    return matrix


def kernel(
    geno, cov, trait, weights, out,
    unit, line, abuf, bbuf, covb, tw, pcat, qmat, ysc, hcat, rcat_a, rcat_b, rfull_a, rfull_b,
    tiles, landed, sum_a, sum_b,
    z_send, z_recv, y_send, y_recv, bx_send, bx_recv, ax_send, ax_recv, core_send, core_recv,
    small_send, small_recv, own_sem, out_send, out_recv,
):
    section = lax.axis_index("samp")
    block = lax.axis_index("var")
    l, k = section // 2, section % 2
    h, z, y = block % 2, (block // 2) % 8, block // 16
    same = (h == l).astype(jnp.int32)
    shift = same * k + (1 - same) * h

    def index(yy, zz, hh):
        return ((yy + 16) % 8 * 8 + (zz + 16) % 8) * 2 + hh

    def samp(ll, kk):
        return 2 * ll + kk

    def is_me(target):
        return (target[0] == section) & (target[1] == block)

    def unless_me(target, action):
        pl.when(jnp.logical_not(is_me(target)))(action)

    def send(src, dst, send_sem, recv_sem, target):
        return pltpu.make_async_remote_copy(
            src_ref=src, dst_ref=dst, send_sem=send_sem, recv_sem=recv_sem,
            device_id=target, device_id_type=MESH,
        )

    def send_or_copy(src, dst, send_sem, recv_sem, target):
        mine = is_me(target)
        remote = send(src, dst, send_sem, recv_sem, target)
        pl.when(jnp.logical_not(mine))(remote.start)
        pl.when(mine)(pltpu.make_async_copy(src, dst, recv_sem).start)
        return lambda: unless_me(target, remote.wait_send)

    def landing(ref, sem):
        pltpu.make_async_copy(ref, ref, sem).wait()

    own_part = covb.at[2 * k + l]
    own = [
        pltpu.make_async_copy(cov, own_part.at[: cov.shape[0]], own_sem.at[0]),
        pltpu.make_async_copy(trait, own_part.at[cov.shape[0] :], own_sem.at[1]),
        pltpu.make_async_copy(weights, tw, own_sem.at[2]),
        pltpu.make_async_copy(geno, unit, own_sem.at[3]),
    ]
    for copy in own:
        copy.start()

    peers = [((section + step) % 4, block) for step in range(1, 4)]
    z_targets = [(section, index(y, z - d, h)) for d in ALONG_Z[1:4]]
    z_sources = [(section, index(y, z + d, h)) for d in ALONG_Z[1:4]]
    y_offsets = (0, 1, 7, 2, 6, 3, 5)
    y_targets = {e: (samp(l, e // SIDE), index(y - e, z, h)) for e in y_offsets}
    y_onward = (samp(l, 1), index(y - 2 + 4 * k, z, h))
    z_onward = z_targets[1]
    y_sources = [
        (samp(l, kk), index(y + (4 * k + b if b else k * (2 - 4 * kk)), z, h))
        for b in range(SIDE)
        for kk in range(2)
    ]
    beside = (samp(1 - l, k), block)
    sibling = (samp(l, 1 - k), block)
    ax_targets = [(samp(h, k), index(y, z, hh)) for hh in range(2)]
    ax_sources = [(samp(ll, k), index(y, z, l)) for ll in range(2)]

    barrier = pltpu.get_barrier_semaphore()
    for source in peers + z_sources + y_sources + [beside, sibling] + ax_sources:
        unless_me(
            source,
            lambda source=source: pl.semaphore_signal(
                barrier, inc=1, device_id=source, device_id_type=MESH
            ),
        )
    for copy in own:
        copy.wait()
    pl.semaphore_wait(barrier, 18 - (1 - k) - same)

    sent = []
    small = []
    for n, peer in enumerate(peers):
        copy = send(own_part, own_part, small_send.at[n], small_recv.at[2 - n], peer)
        copy.start()
        small.append(copy)
    for n in range(3):
        copy = send(unit, line.at[n], z_send.at[n], z_recv.at[n], z_targets[n])
        copy.start()
        sent.append(copy.wait_send)
    for e in y_offsets:
        dst = bbuf.at[e % SIDE, k, l]
        sent.append(send_or_copy(unit, dst, y_send.at[e], y_recv.at[e % SIDE], y_targets[e]))

    def pass_a(slot):
        src = unit if slot == 0 else line.at[slot - 1]
        if slot > 0:
            landing(src, z_recv.at[slot - 1])
        for n, target in enumerate(ax_targets):
            dst = abuf.at[slot, k, l]
            sent.append(send_or_copy(src, dst, ax_send.at[slot, n], ax_recv.at[slot], target))
        if slot == 2:
            copy = send(src, line.at[3], z_send.at[3], z_recv.at[3], z_onward)
            copy.start()
            sent.append(copy.wait_send)

    b_order = (1 + 2 * k, 2, k, 3 - 3 * k)

    def pass_b(step):
        slot = b_order[step]
        half = bbuf.at[slot, :, l]
        landing(half, y_recv.at[slot])
        copy = send(half, half, bx_send.at[step], bx_recv.at[slot], beside)
        copy.start()
        sent.append(copy.wait_send)
        if step == 1:
            copy = send(bbuf.at[2, k, l], bbuf.at[0, k, l], y_send.at[4], y_recv.at[0], y_onward)
            copy.start()
            sent.append(copy.wait_send)

    def pass_core(slot):
        part = abuf.at[slot, k]
        landing(part, ax_recv.at[slot])
        copy = send(part, part, core_send.at[slot], core_recv.at[slot], sibling)
        copy.start()
        sent.append(copy.wait_send)

    pass_a(0)
    for copy in small:
        copy.wait()
    both = jnp.concatenate([covb[n] for n in range(4)], axis=1)
    cov_t, trait_t = both[: cov.shape[0]], both[cov.shape[0] :]
    width, count = cov_t.shape
    eye = (
        lax.broadcasted_iota(jnp.int32, (width, width), 0)
        == lax.broadcasted_iota(jnp.int32, (width, width), 1)
    ).astype(jnp.float32)
    swept = dot(cov_t, cov_t, ((1,), (1,)), HIGHEST) + count / 10.0 * eye
    pass_a(1)
    pass_b(0)
    pass_a(2)
    pass_b(1)
    swept = sweep(swept, 0, 12)
    pass_core(0)
    pass_b(2)
    swept = sweep(swept, 12, 20)
    pass_a(3)
    pass_core(1)
    swept = sweep(swept, 20, 28)
    pass_core(2)
    pass_a(4)
    swept = sweep(swept, 28, width)
    pass_b(3)
    pass_core(3)
    solved = dot(-swept, cov_t, precision=HIGHEST)
    hat = dot(cov_t, solved, ((0,), (0,)), HIGHEST)
    diagonal = lax.broadcasted_iota(jnp.int32, (count, count), 0) == lax.broadcasted_iota(
        jnp.int32, (count, count), 1
    )
    project = jnp.where(diagonal, 1.0, 0.0) - hat
    high, low = split(project)
    pcat[:, :count] = high
    pcat[:, count:] = low
    scaled = dot(trait_t, project, precision=HIGHEST) * (1.0 / math.sqrt(count))
    ysc[...] = scaled
    traits_id = lax.broadcasted_iota(jnp.int32, (scaled.shape[0], 1), 0)
    tw_col = sum(jnp.where(traits_id == t, tw[t], 0.0) for t in range(scaled.shape[0]))
    qmat[...] = dot(scaled * tw_col, scaled, ((0,), (0,)), HIGHEST)
    def prepare(genotypes, ats, rcat, rfull, hrows):
        genotypes = [g.astype(jnp.float32).reshape(count, 128) for g in genotypes]
        centred = (jnp.concatenate(genotypes, axis=1) - 1.0).astype(jnp.bfloat16)
        resids = dot(pcat[...], jnp.concatenate([centred, centred], axis=0))
        for n, (at, hrow) in enumerate(zip(ats, hrows)):
            resid = resids[:, n * 128 : (n + 1) * 128]
            high, low = split(resid)
            at = pl.ds(pl.multiple_of(at * 128, 128), 128)
            rfull[:, at] = 2.0 * resid - high.astype(jnp.float32)
            rcat[:count, at] = high
            rcat[count:, at] = high
            gram = dot(
                jnp.concatenate([high, low + low], axis=1),
                jnp.concatenate([high, high], axis=1),
                ((1,), (1,)),
            )
            h_high, h_low = split(gram * qmat[...])
            rows = pl.ds(pl.multiple_of(hrow * count, count), count)
            hcat[rows, :count] = h_high
            hcat[rows, count:] = h_low

    def prepare_b(first):
        slots = [first, first + 1]
        for slot in slots:
            landing(bbuf.at[slot, :, 1 - l], bx_recv.at[slot])
        hrows = [A_SLOTS + slot for slot in slots]
        prepare([bbuf[slot] for slot in slots], slots, rcat_b, rfull_b, hrows)

    def prepare_a(*slots):
        for slot in slots:
            landing(abuf.at[slot, 1 - k], core_recv.at[slot])
        prepare([abuf[slot] for slot in slots], slots, rcat_a, rfull_a, slots)

    def pairs(hrow, number, rcat, rfull, at):
        at = pl.ds(pl.multiple_of(at * 128, 128), 256)
        rows = pl.ds(pl.multiple_of(hrow * count, count), number * count)
        product = dot(hcat[rows, :], rcat[:, at])
        weighted = product.reshape(number, count, 256) * rfull[:, at][None]
        sums = jnp.sum(weighted, axis=1)
        return jnp.concatenate([sums, jnp.zeros((8 - number, 256), jnp.float32)], axis=0)

    row_ids = lax.broadcasted_iota(jnp.int32, (8, 128), 0)

    def give_back(slot):
        if slot < SIDE:
            offset = jnp.where(shift == 0, ALONG_Z[slot], ALONG_Z[slot + 1])
            owner, at, kind = index(y, z + offset, l), h * 8 + k * 4 + slot, 0
        else:
            owner, at, kind = index(y + 4 * k + slot - SIDE, z, h), 16 + l * 8 + k * 4 + slot - SIDE, 1
        for q in range(4):
            sem = out_send.at[slot * 4 + q]
            sent.append(
                send_or_copy(tiles.at[slot], landed.at[at], sem, out_recv.at[kind], (q, owner))
            )

    def score_a(part):
        sums = pltpu.roll(pairs(A_SLOTS, SIDE, rcat_a, rfull_a, shift + 2 * part), 4 * k, 0)
        tiles[2 * part] = sums[:, :128]
        tiles[2 * part + 1] = sums[:, 128:]

    def score_b(part, of_a):
        sums = pairs(shift + 2 * of_a, 2, rcat_b, rfull_b, 2 * part)
        sums = pltpu.roll(sums, shift + 2 * of_a, 0)
        picked = [sums[a : a + 1] for a in (0, 1, 2, 5, 4, 3, 6, 7)]
        sums = jnp.concatenate(picked, axis=0)
        for n in range(2):
            at, half = SIDE + 2 * part + n, sums[:, n * 128 : (n + 1) * 128]
            tiles[at] = tiles[at] + half if of_a else half

    prepare_b(2 * k)
    prepare_a(0, 1)
    pass_core(4)
    prepare_b(2 - 2 * k)
    prepare_a(2)
    score_a(0)

    @pl.when((same == 1) & (k == 0))
    def _():
        resid = 0.5 * (rfull_a[:, :128] + rcat_a[:count, :128].astype(jnp.float32))
        diag = dot(ysc[...], resid * resid, precision=HIGHEST)
        diag = jnp.sum(diag * diag * tw_col, axis=0, keepdims=True)
        tiles[0] = tiles[0] - jnp.where(row_ids == 0, diag, 0.0)

    give_back(1)
    give_back(0)
    score_b(0, 0)
    score_b(1, 0)
    prepare_a(3, 4)
    score_a(1)
    give_back(3)
    give_back(2)
    score_b(1, 1)
    give_back(7)
    give_back(6)
    score_b(0, 1)

    @pl.when(same == 1)
    def _():
        rows = pl.ds(pl.multiple_of((1 - k) * 4 * count, count), count)
        product = dot(hcat[rows, :], rcat_b[:, :128])
        extra = jnp.sum(product * rfull_b[:, :128], axis=0, keepdims=True)
        tile = jnp.where(row_ids == 4 * k, 0.0, tiles[SIDE])
        tiles[SIDE] = jnp.where(row_ids == 4 * (1 - k), extra, tile)

    give_back(4)
    give_back(5)

    sum_a[...] = jnp.zeros_like(sum_a)
    landing(landed.at[:16], out_recv.at[0])
    for i in range(2):
        mixed = jnp.not_equal(h, i).astype(jnp.int32)
        for kk in range(2):
            first = mixed * (1 - h) + (1 - mixed) * kk
            for n in range(SIDE):
                offset = jnp.where(first == 0, ALONG_Z[n], ALONG_Z[n + 1])
                there = pl.ds((z + 8 - offset) % 8 * 2 + i, 8, stride=16)
                sum_a[there, :] = sum_a[there, :] + pltpu.roll(landed[i * 8 + kk * 4 + n], y, 0)
    landing(landed.at[16:], out_recv.at[1])
    for i in range(2):
        for e in range(8):
            there = pl.ds((y + 8 - e) % 8 * 16 + i, 8, stride=2)
            sum_b[there, :] = pltpu.roll(landed[16 + i * 8 + e], z, 0)
    for wait in sent:
        wait()
    out[...] = (sum_a[...] + sum_b[...]).T * (1.0 / out.shape[0])


def body(genotypes, covariates, traits, trait_weights):
    part, width = genotypes.shape
    count = 4 * part
    cov_count, trait_count = covariates.shape[1], traits.shape[1]
    f32, bf16, i32 = jnp.float32, jnp.bfloat16, jnp.int32
    dma = pltpu.SemaphoreType.DMA
    inputs = (genotypes, covariates.T, traits.T, trait_weights)
    held = [pltpu.with_memory_space_constraint(value, pltpu.HBM) for value in inputs]
    return pl.pallas_call(
        kernel,
        name="epistasis",
        out_shape=jax.ShapeDtypeStruct((width, 128), f32),
        in_specs=[pl.BlockSpec(memory_space=pl.ANY)] * 4,
        out_specs=pl.BlockSpec(memory_space=pltpu.VMEM),
        scratch_shapes=[
            pltpu.VMEM((part, width), i32),
            pltpu.VMEM((A_SLOTS - 1, part, width), i32),
            pltpu.VMEM((A_SLOTS, 2, 2, part, width), i32),
            pltpu.VMEM((SIDE, 2, 2, part, width), i32),
            pltpu.VMEM((4, cov_count + trait_count, part), f32),
            pltpu.SMEM((trait_count,), f32),
            pltpu.VMEM((count, 2 * count), bf16),
            pltpu.VMEM((count, count), f32),
            pltpu.VMEM((trait_count, count), f32),
            pltpu.VMEM(((A_SLOTS + SIDE) * count, 2 * count), bf16),
            pltpu.VMEM((2 * count, A_SLOTS * width), bf16),
            pltpu.VMEM((2 * count, SIDE * width), bf16),
            pltpu.VMEM((count, A_SLOTS * width), f32),
            pltpu.VMEM((count, SIDE * width), f32),
            pltpu.VMEM((2 * SIDE, 8, width), f32),
            pltpu.VMEM((32, 8, width), f32),
            pltpu.VMEM((128, width), f32),
            pltpu.VMEM((128, width), f32),
            dma((4,)), dma((4,)), dma((8,)), dma((SIDE,)), dma((SIDE,)), dma((SIDE,)),
            dma((A_SLOTS, 2)), dma((A_SLOTS,)), dma((A_SLOTS,)), dma((A_SLOTS,)),
            dma((3,)), dma((3,)), dma((4,)), dma((32,)), dma((2,)),
        ],
        compiler_params=pltpu.CompilerParams(
            collective_id=0, has_side_effects=True, vmem_limit_bytes=32 << 20
        ),
    )(*held)


def solution(mesh):
    placed = (P("samp", "var"), P("samp", None), P("samp", None), P())
    return jax.shard_map(
        body, mesh=mesh, in_specs=placed, out_specs=P("var", None), check_vma=False
    )
```

time: 47.5 us -> 40.1 us (0.84)
  Pallas kernels: 45.9 us -> 39.2 us
  local copies, waits for them, and re-layouts: 1.47 us -> 0.63 us
    pallas_call x1, Pallas kernels: 45.9 us -> 39.2 us  [body(): pl.pallas_call(kernel, name='epistasis', out_shape=jax.ShapeDtypeStruct((...]
    unnamed x1, local copies, waits for them, and re-layouts: 1.47 us -> 0.63 us
where the time goes in v3:
time: 40.1 us; the launch traced here: 39.9 us
  Pallas kernels  39.2 us (98%)
  local copies, waits for them, and re-layouts  0.63 us (2%)
    pallas_call x1, Pallas kernels, body(): pl.pallas_call(kernel, name='epistasis', out_shape=jax.ShapeDtypeStruct((...  39.2 us

profile of v3, /device:TPU:1, one launch (start us, length us, event | category | flops | bytes accessed | tf_op | source)
XLA Modules:
  0.0 39.9 jit_solution(14681090638332627740)
XLA Ops:
  0.0 39.2 %epistasis.1 = f32[128,128]{1,0:T(8,128)S(1)} custom-call(s32[64,128]{1,0:T(8,128)} %geno.1, f32[40,64]{1,0:T(8,128)} %bitcast.2, f32[8,64]{1,0:T(8,128)} %bitcast.3, f32[8]{0:T(128)} %weights.1), custom_call_target="tpu_custom_call" | custom-call | tf_op jit(solution)/shard_map/epistasis/pallas_call | solution.py:354
  39.2 0.6 %copy.6 = f32[128,128]{1,0:T(8,128)} copy(f32[128,128]{1,0:T(8,128)S(1)} %epistasis.1) | data formatting | bytes 131072

commit v4 on v3

--- a/solution.py
+++ b/solution.py
@@ -10,7 +10,7 @@
 MESH = pl.DeviceIdType.MESH
 HIGHEST = lax.Precision.HIGHEST
 SIDE = 4
-ALONG_Z = (0, 1, 2, -3, 4)
+ALONG_Z = (0, -1, -2, 3, 4)
 A_SLOTS = len(ALONG_Z)
 
 
@@ -31,11 +31,12 @@
     cols = lax.broadcasted_iota(jnp.int32, (size, size), 1)
     for k in range(begin, end, 2):
         row_1, row_2 = matrix[k : k + 1, :], matrix[k + 1 : k + 2, :]
-        col_1, col_2 = matrix[:, k : k + 1], matrix[:, k + 1 : k + 2]
-        p, q, r = row_1[:, k : k + 1], row_1[:, k + 1 : k + 2], row_2[:, k + 1 : k + 2]
+        col_1 = jnp.broadcast_to(matrix[:, k : k + 1], (size, size))
+        col_2 = jnp.broadcast_to(matrix[:, k + 1 : k + 2], (size, size))
+        p, q, r = col_1[k : k + 1, :], col_2[k : k + 1, :], col_2[k + 1 : k + 2, :]
         scale = 1.0 / (p * r - q * q)
-        row_1 = jnp.where(cols == k, -1.0, jnp.where(cols == k + 1, 0.0, row_1))
-        row_2 = jnp.where(cols == k + 1, -1.0, jnp.where(cols == k, 0.0, row_2))
+        row_1 = jnp.where(cols[:1] == k, -1.0, jnp.where(cols[:1] == k + 1, 0.0, row_1))
+        row_2 = jnp.where(cols[:1] == k + 1, -1.0, jnp.where(cols[:1] == k, 0.0, row_2))
         col_1 = jnp.where(rows == k, -1.0, jnp.where(rows == k + 1, 0.0, col_1))
         col_2 = jnp.where(rows == k + 1, -1.0, jnp.where(rows == k, 0.0, col_2))
         kept = (rows == k) | (rows == k + 1) | (cols == k) | (cols == k + 1)
@@ -62,7 +63,7 @@
     shift = same * k + (1 - same) * h
 
     def index(yy, zz, hh):
-        return ((yy + 16) % 8 * 8 + (zz + 16) % 8) * 2 + hh
+        return (lax.rem(yy + 16, 8) * 8 + lax.rem(zz + 16, 8)) * 2 + hh
 
     def samp(ll, kk):
         return 2 * ll + kk
@@ -85,6 +86,11 @@
         pl.when(jnp.logical_not(mine))(remote.start)
         pl.when(mine)(pltpu.make_async_copy(src, dst, recv_sem).start)
         return lambda: unless_me(target, remote.wait_send)
+
+    def send_on(src, dst, send_sem, recv_sem, target):
+        remote = send(src, dst, send_sem, recv_sem, target)
+        remote.start()
+        return remote.wait_send
 
     def landing(ref, sem):
         pltpu.make_async_copy(ref, ref, sem).wait()
@@ -100,12 +106,17 @@
         copy.start()
 
     peers = [((section + step) % 4, block) for step in range(1, 4)]
-    z_targets = [(section, index(y, z - d, h)) for d in ALONG_Z[1:4]]
-    z_sources = [(section, index(y, z + d, h)) for d in ALONG_Z[1:4]]
+    z_targets = [(section, index(y, z - d, h)) for d in ALONG_Z[2:4]]
+    z_sources = [(section, index(y, z + d, h)) for d in ALONG_Z[2:4]]
+    a1_targets = [(samp(h, k), index(y, z - ALONG_Z[1], hh)) for hh in range(2)]
+    a1_sources = [(samp(ll, k), index(y, z + ALONG_Z[1], l)) for ll in range(2)]
+    y_across = {e: (samp(1 - l, e // SIDE), index(y - e, z, h)) for e in (0, 1, 7)}
+    y_across_sources = [(samp(1 - l, kk), index(y + 7 * k, z, h)) for kk in range(2)]
+    y_across_core_0 = [(samp(1 - l, kk), index(y + 1, z, h)) for kk in range(2)]
     y_offsets = (0, 1, 7, 2, 6, 3, 5)
     y_targets = {e: (samp(l, e // SIDE), index(y - e, z, h)) for e in y_offsets}
     y_onward = (samp(l, 1), index(y - 2 + 4 * k, z, h))
-    z_onward = z_targets[1]
+    z_onward = z_targets[0]
     y_sources = [
         (samp(l, kk), index(y + (4 * k + b if b else k * (2 - 4 * kk)), z, h))
         for b in range(SIDE)
@@ -115,9 +126,28 @@
     sibling = (samp(l, 1 - k), block)
     ax_targets = [(samp(h, k), index(y, z, hh)) for hh in range(2)]
     ax_sources = [(samp(ll, k), index(y, z, l)) for ll in range(2)]
+    a4_across = [(samp(h, 1 - k), index(y, z, hh)) for hh in range(2)]
+    a4_across_sources = [(samp(ll, 1 - k), index(y, z, l)) for ll in range(2)]
+
+    owners = []
+    for slot in range(SIDE):
+        offset = jnp.where(shift == 0, ALONG_Z[slot], ALONG_Z[slot + 1])
+        owners.append((index(y, z + offset, l), h * 8 + k * 4 + slot))
+    for slot in range(SIDE):
+        owners.append((index(y + 4 * k + slot, z, h), 16 + l * 8 + k * 4 + slot))
 
     barrier = pltpu.get_barrier_semaphore()
-    for source in peers + z_sources + y_sources + [beside, sibling] + ax_sources:
+    for source in peers + z_sources + y_sources[1:] + [beside, sibling] + a4_across_sources + (
+        a1_sources + y_across_sources
+    ):
+        pl.semaphore_signal(barrier, inc=1, device_id=source, device_id_type=MESH)
+    for source in y_across_core_0:
+        pl.when(k == 0)(
+            lambda source=source: pl.semaphore_signal(
+                barrier, inc=1, device_id=source, device_id_type=MESH
+            )
+        )
+    for source in [y_sources[0]] + ax_sources:
         unless_me(
             source,
             lambda source=source: pl.semaphore_signal(
@@ -126,7 +156,7 @@
         )
     for copy in own:
         copy.wait()
-    pl.semaphore_wait(barrier, 18 - (1 - k) - same)
+    pl.semaphore_wait(barrier, 24 - (1 - k) - same)
 
     sent = []
     small = []
@@ -134,21 +164,47 @@
         copy = send(own_part, own_part, small_send.at[n], small_recv.at[2 - n], peer)
         copy.start()
         small.append(copy)
-    for n in range(3):
-        copy = send(unit, line.at[n], z_send.at[n], z_recv.at[n], z_targets[n])
-        copy.start()
-        sent.append(copy.wait_send)
-    for e in y_offsets:
-        dst = bbuf.at[e % SIDE, k, l]
-        sent.append(send_or_copy(unit, dst, y_send.at[e], y_recv.at[e % SIDE], y_targets[e]))
+
+    def send_y(e):
+        slot = e % SIDE
+        deliver = send_or_copy if e == 0 else send_on
+        dst = bbuf.at[slot, k, l]
+        sent.append(deliver(unit, dst, y_send.at[e], y_recv.at[slot], y_targets[e]))
+        if e in y_across:
+            sem = y_send.at[8 + e]
+            sent.append(send_on(unit, dst, sem, bx_recv.at[slot], y_across[e]))
+
+    def send_z(n):
+        sem = z_send.at[n]
+        sent.append(send_on(unit, line.at[n], sem, z_recv.at[n], z_targets[n - 1]))
+
+    def send_slot(slot, targets):
+        for n, target in enumerate(targets):
+            deliver = send_or_copy if slot == 0 else send_on
+            dst, sem = abuf.at[slot, k, l], ax_send.at[slot, n]
+            sent.append(deliver(unit, dst, sem, ax_recv.at[slot], target))
+
+    send_y(1)
+    send_y(7)
+    send_slot(1, a1_targets)
+    send_slot(0, ax_targets)
+    send_z(1)
+    send_y(2)
+    send_y(6)
+    send_y(0)
+    send_z(2)
+    send_y(3)
+    send_y(5)
 
     def pass_a(slot):
-        src = unit if slot == 0 else line.at[slot - 1]
-        if slot > 0:
-            landing(src, z_recv.at[slot - 1])
+        src = line.at[slot - 1]
+        landing(src, z_recv.at[slot - 1])
         for n, target in enumerate(ax_targets):
             dst = abuf.at[slot, k, l]
             sent.append(send_or_copy(src, dst, ax_send.at[slot, n], ax_recv.at[slot], target))
+            if slot == 4:
+                sem, sem_there = ax_send.at[slot, 2 + n], core_recv.at[slot]
+                sent.append(send_on(src, dst, sem, sem_there, a4_across[n]))
         if slot == 2:
             copy = send(src, line.at[3], z_send.at[3], z_recv.at[3], z_onward)
             copy.start()
@@ -160,9 +216,15 @@
         slot = b_order[step]
         half = bbuf.at[slot, :, l]
         landing(half, y_recv.at[slot])
+        if step == 0:
+            return
         copy = send(half, half, bx_send.at[step], bx_recv.at[slot], beside)
-        copy.start()
-        sent.append(copy.wait_send)
+        if step == 2:
+            pl.when(k == 1)(copy.start)
+            sent.append(lambda: pl.when(k == 1)(copy.wait_send))
+        else:
+            copy.start()
+            sent.append(copy.wait_send)
         if step == 1:
             copy = send(bbuf.at[2, k, l], bbuf.at[0, k, l], y_send.at[4], y_recv.at[0], y_onward)
             copy.start()
@@ -175,7 +237,6 @@
         copy.start()
         sent.append(copy.wait_send)
 
-    pass_a(0)
     for copy in small:
         copy.wait()
     both = jnp.concatenate([covb[n] for n in range(4)], axis=1)
@@ -186,22 +247,16 @@
         == lax.broadcasted_iota(jnp.int32, (width, width), 1)
     ).astype(jnp.float32)
     swept = dot(cov_t, cov_t, ((1,), (1,)), HIGHEST) + count / 10.0 * eye
-    pass_a(1)
-    pass_b(0)
     pass_a(2)
     pass_b(1)
-    swept = sweep(swept, 0, 12)
+    swept = sweep(swept, 0, 20)
     pass_core(0)
     pass_b(2)
-    swept = sweep(swept, 12, 20)
     pass_a(3)
     pass_core(1)
-    swept = sweep(swept, 20, 28)
+    swept = sweep(swept, 20, width)
     pass_core(2)
-    pass_a(4)
-    swept = sweep(swept, 28, width)
-    pass_b(3)
-    pass_core(3)
+    pass_b(0)
     solved = dot(-swept, cov_t, precision=HIGHEST)
     hat = dot(cov_t, solved, ((0,), (0,)), HIGHEST)
     diagonal = lax.broadcasted_iota(jnp.int32, (count, count), 0) == lax.broadcasted_iota(
@@ -211,11 +266,14 @@
     high, low = split(project)
     pcat[:, :count] = high
     pcat[:, count:] = low
+    pass_a(4)
+    pass_b(3)
     scaled = dot(trait_t, project, precision=HIGHEST) * (1.0 / math.sqrt(count))
     ysc[...] = scaled
     traits_id = lax.broadcasted_iota(jnp.int32, (scaled.shape[0], 1), 0)
     tw_col = sum(jnp.where(traits_id == t, tw[t], 0.0) for t in range(scaled.shape[0]))
     qmat[...] = dot(scaled * tw_col, scaled, ((0,), (0,)), HIGHEST)
+    pass_core(3)
     def prepare(genotypes, ats, rcat, rfull, hrows):
         genotypes = [g.astype(jnp.float32).reshape(count, 128) for g in genotypes]
         centred = (jnp.concatenate(genotypes, axis=1) - 1.0).astype(jnp.bfloat16)
@@ -246,6 +304,8 @@
 
     def prepare_a(*slots):
         for slot in slots:
+            if slot == 4:
+                landing(abuf.at[slot, k], ax_recv.at[slot])
             landing(abuf.at[slot, 1 - k], core_recv.at[slot])
         prepare([abuf[slot] for slot in slots], slots, rcat_a, rfull_a, slots)
 
@@ -260,37 +320,40 @@
     row_ids = lax.broadcasted_iota(jnp.int32, (8, 128), 0)
 
     def give_back(slot):
-        if slot < SIDE:
-            offset = jnp.where(shift == 0, ALONG_Z[slot], ALONG_Z[slot + 1])
-            owner, at, kind = index(y, z + offset, l), h * 8 + k * 4 + slot, 0
-        else:
-            owner, at, kind = index(y + 4 * k + slot - SIDE, z, h), 16 + l * 8 + k * 4 + slot - SIDE, 1
+        owner, at = owners[slot]
         for q in range(4):
             sem = out_send.at[slot * 4 + q]
-            sent.append(
-                send_or_copy(tiles.at[slot], landed.at[at], sem, out_recv.at[kind], (q, owner))
-            )
-
-    def score_a(part):
-        sums = pltpu.roll(pairs(A_SLOTS, SIDE, rcat_a, rfull_a, shift + 2 * part), 4 * k, 0)
-        tiles[2 * part] = sums[:, :128]
-        tiles[2 * part + 1] = sums[:, 128:]
-
-    def score_b(part, of_a):
-        sums = pairs(shift + 2 * of_a, 2, rcat_b, rfull_b, 2 * part)
+            deliver = send_or_copy if slot in (0, SIDE) else send_on
+            kind = out_recv.at[slot // SIDE]
+            sent.append(deliver(tiles.at[slot], landed.at[at], sem, kind, (q, owner)))
+
+    near, rest = 2 * k, 2 - 2 * k
+
+    def add(at, part, fresh):
+        tiles[at] = part if fresh else tiles[at] + part
+
+    def score_a(part, number, first, fresh):
+        sums = pairs(A_SLOTS + first, number, rcat_a, rfull_a, shift + 2 * part)
+        sums = pltpu.roll(sums, 4 * k + first, 0)
+        add(2 * part, sums[:, :128], fresh)
+        add(2 * part + 1, sums[:, 128:], fresh)
+
+    def score_b(first, of_a, number, fresh):
+        sums = pairs(shift + 2 * of_a, number, rcat_b, rfull_b, first)
         sums = pltpu.roll(sums, shift + 2 * of_a, 0)
-        picked = [sums[a : a + 1] for a in (0, 1, 2, 5, 4, 3, 6, 7)]
+        picked = [sums[a : a + 1] for a in (0, 5, 6, 3, 4, 7, 2, 1)]
         sums = jnp.concatenate(picked, axis=0)
-        for n in range(2):
-            at, half = SIDE + 2 * part + n, sums[:, n * 128 : (n + 1) * 128]
-            tiles[at] = tiles[at] + half if of_a else half
-
-    prepare_b(2 * k)
+        add(SIDE + first, sums[:, :128], fresh)
+        add(SIDE + first + 1, sums[:, 128:], fresh)
+
+    prepare_b(near)
     prepare_a(0, 1)
-    pass_core(4)
-    prepare_b(2 - 2 * k)
     prepare_a(2)
-    score_a(0)
+    score_a(0, 2, near, True)
+    score_b(near, 0, 2, True)
+    prepare_b(rest)
+    score_a(0, 2, rest, False)
+    score_b(rest, 0, 2, True)
 
     @pl.when((same == 1) & (k == 0))
     def _():
@@ -301,16 +364,14 @@
 
     give_back(1)
     give_back(0)
-    score_b(0, 0)
-    score_b(1, 0)
     prepare_a(3, 4)
-    score_a(1)
+    score_a(1, 4, 0, True)
     give_back(3)
     give_back(2)
-    score_b(1, 1)
+    score_b(2, 1, 2, False)
     give_back(7)
     give_back(6)
-    score_b(0, 1)
+    score_b(0, 1, 2, False)
 
     @pl.when(same == 1)
     def _():
@@ -324,6 +385,8 @@
     give_back(5)
 
     sum_a[...] = jnp.zeros_like(sum_a)
+    for wait in sent:
+        wait()
     landing(landed.at[:16], out_recv.at[0])
     for i in range(2):
         mixed = jnp.not_equal(h, i).astype(jnp.int32)
@@ -338,8 +401,6 @@
         for e in range(8):
             there = pl.ds((y + 8 - e) % 8 * 16 + i, 8, stride=2)
             sum_b[there, :] = pltpu.roll(landed[16 + i * 8 + e], z, 0)
-    for wait in sent:
-        wait()
     out[...] = (sum_a[...] + sum_b[...]).T * (1.0 / out.shape[0])
 
 
@@ -376,8 +437,8 @@
             pltpu.VMEM((32, 8, width), f32),
             pltpu.VMEM((128, width), f32),
             pltpu.VMEM((128, width), f32),
-            dma((4,)), dma((4,)), dma((8,)), dma((SIDE,)), dma((SIDE,)), dma((SIDE,)),
-            dma((A_SLOTS, 2)), dma((A_SLOTS,)), dma((A_SLOTS,)), dma((A_SLOTS,)),
+            dma((4,)), dma((4,)), dma((16,)), dma((SIDE,)), dma((SIDE,)), dma((SIDE,)),
+            dma((A_SLOTS, 4)), dma((A_SLOTS,)), dma((A_SLOTS,)), dma((A_SLOTS,)),
             dma((3,)), dma((3,)), dma((4,)), dma((32,)), dma((2,)),
         ],
         compiler_params=pltpu.CompilerParams(

time: 40.1 us -> 38.8 us (0.968)
  Pallas kernels: 39.2 us -> 38 us
    pallas_call x1, Pallas kernels: 39.2 us -> 38 us  [body(): pl.pallas_call(kernel, name='epistasis', out_shape=jax.ShapeDtypeStruct((...]
where the time goes in v4:
time: 38.8 us; the launch traced here: 38.7 us
  Pallas kernels  38 us (98%)
  local copies, waits for them, and re-layouts  0.63 us (2%)
    pallas_call x1, Pallas kernels, body(): pl.pallas_call(kernel, name='epistasis', out_shape=jax.ShapeDtypeStruct((...  38 us

profile of v4, /device:TPU:1, one launch (start us, length us, event | category | flops | bytes accessed | tf_op | source)
XLA Modules:
  0.0 38.7 jit_solution(2170518672984381530)
XLA Ops:
  0.0 38.0 %epistasis.1 = f32[128,128]{1,0:T(8,128)S(1)} custom-call(s32[64,128]{1,0:T(8,128)} %geno.1, f32[40,64]{1,0:T(8,128)} %bitcast.2, f32[8,64]{1,0:T(8,128)} %bitcast.3, f32[8]{0:T(128)} %weights.1), custom_call_target="tpu_custom_call" | custom-call | tf_op jit(solution)/shard_map/epistasis/pallas_call | solution.py:415
  38.0 0.6 %copy.6 = f32[128,128]{1,0:T(8,128)} copy(f32[128,128]{1,0:T(8,128)S(1)} %epistasis.1) | data formatting | bytes 131072

commit v5 on v4

--- a/solution.py
+++ b/solution.py
@@ -257,6 +257,8 @@
     swept = sweep(swept, 20, width)
     pass_core(2)
     pass_b(0)
+    pass_a(4)
+    pass_b(3)
     solved = dot(-swept, cov_t, precision=HIGHEST)
     hat = dot(cov_t, solved, ((0,), (0,)), HIGHEST)
     diagonal = lax.broadcasted_iota(jnp.int32, (count, count), 0) == lax.broadcasted_iota(
@@ -266,8 +268,6 @@
     high, low = split(project)
     pcat[:, :count] = high
     pcat[:, count:] = low
-    pass_a(4)
-    pass_b(3)
     scaled = dot(trait_t, project, precision=HIGHEST) * (1.0 / math.sqrt(count))
     ysc[...] = scaled
     traits_id = lax.broadcasted_iota(jnp.int32, (scaled.shape[0], 1), 0)

time: 38.8 us -> 38.4 us (0.990)
  Pallas kernels: 38 us -> 37.5 us
    pallas_call x1, Pallas kernels: 38 us -> 37.5 us  [body(): pl.pallas_call(kernel, name='epistasis', out_shape=jax.ShapeDtypeStruct((...]
where the time goes in v5:
time: 38.4 us; the launch traced here: 38.2 us
  Pallas kernels  37.5 us (98%)
  local copies, waits for them, and re-layouts  0.63 us (2%)
    pallas_call x1, Pallas kernels, body(): pl.pallas_call(kernel, name='epistasis', out_shape=jax.ShapeDtypeStruct((...  37.5 us

profile of v5, /device:TPU:1, one launch (start us, length us, event | category | flops | bytes accessed | tf_op | source)
XLA Modules:
  0.0 38.2 jit_solution(4963461243171920450)
XLA Ops:
  0.0 37.5 %epistasis.1 = f32[128,128]{1,0:T(8,128)S(1)} custom-call(s32[64,128]{1,0:T(8,128)} %geno.1, f32[40,64]{1,0:T(8,128)} %bitcast.2, f32[8,64]{1,0:T(8,128)} %bitcast.3, f32[8]{0:T(128)} %weights.1), custom_call_target="tpu_custom_call" | custom-call | tf_op jit(solution)/shard_map/epistasis/pallas_call | solution.py:415
  37.5 0.6 %copy.6 = f32[128,128]{1,0:T(8,128)} copy(f32[128,128]{1,0:T(8,128)S(1)} %epistasis.1) | data formatting | bytes 131072

commit v6 on v5

--- a/solution.py
+++ b/solution.py
@@ -384,7 +384,7 @@
     give_back(4)
     give_back(5)
 
-    sum_a[...] = jnp.zeros_like(sum_a)
+    sum_a[:128, :] = jnp.zeros((128, 128), jnp.float32)
     for wait in sent:
         wait()
     landing(landed.at[:16], out_recv.at[0])
@@ -401,7 +401,7 @@
         for e in range(8):
             there = pl.ds((y + 8 - e) % 8 * 16 + i, 8, stride=2)
             sum_b[there, :] = pltpu.roll(landed[16 + i * 8 + e], z, 0)
-    out[...] = (sum_a[...] + sum_b[...]).T * (1.0 / out.shape[0])
+    out[...] = (sum_a[:128, :] + sum_b[:128, :]).T * (1.0 / out.shape[0])
 
 
 def body(genotypes, covariates, traits, trait_weights):
@@ -435,8 +435,8 @@
             pltpu.VMEM((count, SIDE * width), f32),
             pltpu.VMEM((2 * SIDE, 8, width), f32),
             pltpu.VMEM((32, 8, width), f32),
-            pltpu.VMEM((128, width), f32),
-            pltpu.VMEM((128, width), f32),
+            pltpu.VMEM((256, width), f32),
+            pltpu.VMEM((256, width), f32),
             dma((4,)), dma((4,)), dma((16,)), dma((SIDE,)), dma((SIDE,)), dma((SIDE,)),
             dma((A_SLOTS, 4)), dma((A_SLOTS,)), dma((A_SLOTS,)), dma((A_SLOTS,)),
             dma((3,)), dma((3,)), dma((4,)), dma((32,)), dma((2,)),

time: 38.4 us -> 38.4 us (level)
  no operation moved by 1% of the time
where the time goes in v6:
time: 38.4 us; the launch traced here: 38.2 us
  Pallas kernels  37.5 us (98%)
  local copies, waits for them, and re-layouts  0.63 us (2%)
    pallas_call x1, Pallas kernels, body(): pl.pallas_call(kernel, name='epistasis', out_shape=jax.ShapeDtypeStruct((...  37.5 us

profile of v6, /device:TPU:1, one launch (start us, length us, event | category | flops | bytes accessed | tf_op | source)
XLA Modules:
  0.0 38.2 jit_solution(14651768185279823611)
XLA Ops:
  0.0 37.5 %epistasis.1 = f32[128,128]{1,0:T(8,128)S(1)} custom-call(s32[64,128]{1,0:T(8,128)} %geno.1, f32[40,64]{1,0:T(8,128)} %bitcast.2, f32[8,64]{1,0:T(8,128)} %bitcast.3, f32[8]{0:T(128)} %weights.1), custom_call_target="tpu_custom_call" | custom-call | tf_op jit(solution)/shard_map/epistasis/pallas_call | solution.py:415
  37.5 0.6 %copy.6 = f32[128,128]{1,0:T(8,128)} copy(f32[128,128]{1,0:T(8,128)S(1)} %epistasis.1) | data formatting | bytes 131072
